TPU v7x, 512 devices: a whole 4x4x16 slice. The times are simulated.
512 devices in a mesh: pipe: 16 (over z_hi, y), expert: 32 (over z_lo, x, core).
Axes of the slice: x: 4, y: 4, z: 16 (z_hi: 4, z_lo: 4; z = z_hi * 4 + z_lo), core: 2. Of those that a mesh axis runs over, the one named last changes fastest.
Arguments:
- act_fwd: bfloat16 [16, 1024, 3584], P('pipe', 'expert'), may hold values from -6 to 6
- cot_bwd: bfloat16 [16, 1024, 3584], P('pipe', 'expert'), may hold values from -6 to 6
- routes_fwd: int32 [16, 1024, 2], P('pipe', 'expert'), may hold values from 0 to 3, all different within a row; in each aligned block of 32 rows (0 to 31, 32 to 63, ..., all dimensions but the last counted through in order) at most 18 rows name the same one
- gates_fwd: float32 [16, 1024, 2], P('pipe', 'expert'), may hold values from 0.1 to 1
- routes_bwd: int32 [16, 1024, 2], P('pipe', 'expert'), may hold values from 0 to 3, all different within a row; in each aligned block of 32 rows (0 to 31, 32 to 63, ..., all dimensions but the last counted through in order) at most 18 rows name the same one
- gates_bwd: float32 [16, 1024, 2], P('pipe', 'expert'), may hold values from 0.1 to 1
- w_in: bfloat16 [16, 2, 3584, 4096], P('pipe', None, None, 'expert'), may hold values from -0.09375 to 0.09375
- w_down: bfloat16 [16, 4096, 3584], P('pipe', 'expert'), may hold values from -0.1875 to 0.1875
- stash: bfloat16 [16, 18432, 128], P('pipe', 'expert'), may hold values from -0.59765625 to 0.59765625
Outputs:
- moe_out: bfloat16 [16, 1024, 3584], P('pipe', 'expert')
- grad_down: bfloat16 [16, 4096, 3584], P('pipe', 'expert')
Inputs may be any that keep to these rules, and one draw needn't show every extreme that they name: `routes_fwd`: in the rows of one device no expert is named by more than 18 rows, a bound that some block reaches; a row names 2 different experts. `routes_bwd`: in the rows of one device no expert is named by more than 18 rows, a bound that some block reaches; a row names 2 different experts.
All inputs are finite; a program needn't handle non-finite values.
Results may differ from a plain program's by a relative error of at most 0.0059.
Values may be sent and summed in bfloat16 or wider, within the bound.
A program may use at most 128 MiB of HBM per device.

v0:
```python
import jax
import jax.numpy as jnp
from jax import lax
from jax.sharding import PartitionSpec as P

EXPERTS = 4
CAP = 18


def passed_along(value, axis, steps):
    count = lax.axis_size(axis)
    pairs = [(source, (source + steps) % count) for source in range(count)]
    return lax.ppermute(value, axis, pairs)


def swapped(block, axis, distance):
    count = lax.axis_size(axis)
    route = []
    for low in range(count):
        high = low | 1 << distance
        if high != low and high < count:
            route += [(low, high), (high, low)]
    return lax.ppermute(block, axis, route)


def slot_positions(routes, tok_dev):
    source_count = routes.shape[0] // tok_dev
    grouped = routes.reshape(source_count, tok_dev, routes.shape[1])
    hit_table = jnp.sum(
        (grouped[..., None] == jnp.arange(EXPERTS, dtype=jnp.int32)).astype(jnp.int32), axis=2
    )
    position = jnp.cumsum(hit_table, axis=1) - hit_table
    return (hit_table, position)


def combine_table(routes, gates, position):
    matches = routes[:, :, None] == jnp.arange(EXPERTS, dtype=jnp.int32)
    weight = jnp.sum(
        jnp.where(matches, gates[:, :, None], jnp.zeros_like(gates[:, :, None])), axis=1
    )
    placed = (position[:, :, None] == jnp.arange(CAP, dtype=jnp.int32)).astype(jnp.float32)
    comb_table = weight[:, :, None] * placed
    return comb_table.reshape(routes.shape[0], EXPERTS * CAP)


def expert_rows(slot_rows, w_in, w_down):
    source_count, capacity, feature_count = slot_rows.shape
    flat_rows = slot_rows.reshape(source_count * capacity, feature_count)
    gate_proj = jnp.dot(flat_rows, w_in[0, 0], preferred_element_type=jnp.float32)
    up_proj = jnp.dot(flat_rows, w_in[0, 1], preferred_element_type=jnp.float32)
    hidden = (jax.nn.silu(gate_proj) * up_proj).astype(jnp.bfloat16)
    partial_value = jnp.dot(hidden, w_down[0], preferred_element_type=jnp.float32).astype(
        jnp.bfloat16
    )
    return partial_value.reshape(source_count, capacity, feature_count)


def return_rows(partial_value):
    return lax.all_to_all(partial_value, "expert", split_axis=0, concat_axis=0, tiled=True)


def shards(act_fwd, cot_bwd, routes_fwd, gates_fwd, routes_bwd, gates_bwd, w_in, w_down, stash):
    tokens = passed_along(act_fwd, "pipe", 1)[0]
    cotangent = passed_along(cot_bwd, "pipe", -1)[0]
    routes_here = routes_fwd[0]
    tok_dev = tokens.shape[0]
    feature_count = tokens.shape[1]
    device_count = lax.axis_size("expert")
    group_size = device_count // EXPERTS
    owner_index = lax.axis_index("expert") // group_size
    hit_table, position = slot_positions(routes_here, tok_dev)
    capacity_ids = jnp.arange(CAP, dtype=jnp.int32)
    token_rows = lax.all_gather(tokens, "expert", axis=0, tiled=True)
    piece_routes = lax.all_gather(routes_here, "expert", axis=0, tiled=True)
    source_count = token_rows.shape[0] // tok_dev
    hit_piece, position_piece = slot_positions(piece_routes, tok_dev)
    select_mask = (jnp.arange(EXPERTS, dtype=jnp.int32) == owner_index).astype(jnp.int32)
    hit_owner = jnp.sum(hit_piece * select_mask, axis=-1)
    position_owner = jnp.sum(position_piece * select_mask, axis=-1)
    selector = (
        (position_owner[:, None, :] == capacity_ids[None, :, None]) & (hit_owner[:, None, :] > 0)
    ).astype(jnp.bfloat16)
    selected = jnp.einsum(
        "nct,ntd->ncd",
        selector,
        token_rows.reshape(source_count, tok_dev, feature_count),
        preferred_element_type=jnp.float32,
    ).astype(jnp.bfloat16)
    returned = return_rows(expert_rows(selected, w_in, w_down))
    summed = jnp.sum(
        returned.astype(jnp.float32).reshape(EXPERTS, group_size, CAP, feature_count), axis=1
    )
    forward_table = combine_table(routes_here, gates_fwd[0], position[0])
    moe_out = jnp.dot(
        forward_table, summed.reshape(EXPERTS * CAP, feature_count), precision=lax.Precision.HIGHEST
    ).astype(jnp.bfloat16)
    routes_back = routes_bwd[0]
    hit_back, position_back = slot_positions(routes_back, tok_dev)
    backward_table = combine_table(routes_back, gates_bwd[0], position_back[0])
    weighted = lax.dot_general(
        backward_table,
        cotangent.astype(jnp.float32),
        (((0,), (0,)), ((), ())),
        precision=lax.Precision.HIGHEST,
    ).astype(jnp.bfloat16)
    outgoing_grads = jnp.repeat(weighted.reshape(EXPERTS, CAP, feature_count), group_size, axis=0)
    arrived_grads = lax.all_to_all(
        outgoing_grads, "expert", split_axis=0, concat_axis=0, tiled=True
    )
    local_grad = lax.dot_general(
        stash[0],
        arrived_grads.reshape(device_count * CAP, feature_count),
        (((0,), (0,)), ((), ())),
        preferred_element_type=jnp.float32,
    )
    own_grad = local_grad.astype(jnp.bfloat16)
    bit_count = lax.axis_size("pipe").bit_length() - 1
    bit_order = list(range(bit_count))
    moved = own_grad
    for bit_index in bit_order:
        moved = swapped(moved, "pipe", bit_index)
    kept_grad = lax.optimization_barrier(own_grad).astype(jnp.float32)
    summed_grad = (kept_grad + moved.astype(jnp.float32)).astype(jnp.bfloat16)
    return (moe_out[None], summed_grad[None])


def solution(mesh):
    in_specs = (
        P("pipe", "expert", None),
        P("pipe", "expert", None),
        P("pipe", "expert", None),
        P("pipe", "expert", None),
        P("pipe", "expert", None),
        P("pipe", "expert", None),
        P("pipe", None, None, "expert"),
        P("pipe", "expert", None),
        P("pipe", "expert", None),
    )
    out_specs = (P("pipe", "expert", None), P("pipe", "expert", None))
    return jax.shard_map(shards, mesh=mesh, in_specs=in_specs, out_specs=out_specs, check_vma=False)
```

profile of v0, /device:TPU:65, one launch (start us, length us, event | category | flops | bytes accessed | tf_op | source)
XLA Modules:
  0.0 573.6 jit_solution(7661251148374156892)
XLA Ops:
  7.2 13.2 %collective-permute-start.1 = (bf16[1,32,3584]{2,1,0:T(8,128)(2,1)}, bf16[1,32,3584]{2,1,0:T(8,128)(2,1)S(1)}, u32[]{:S(2)}, u32[]{:S(2)}) collective-permute-start(bf16[1,32,3584]{2,1,0:T(8,128)(2,1)} %param.10), channel_id=1, source_target_pairs={{0,480},{32,0},{64,32},{96,64},{128,96},{160,128},{192,160},{224,1... | collective-permute-start | bytes 688136 | tf_op jit(solution)/shard_map/ppermute | solution.py:13
  20.4 0.7 select_reduce_fusion
  21.1 0.7 convert_reduce_fusion.2
  21.8 0.1 copy.53
  22.0 0.1 copy.55
  22.1 0.1 fusion.28
  22.2 0.1 mul.48
  22.3 13.9 %collective-permute-done.1 = bf16[1,32,3584]{2,1,0:T(8,128)(2,1)S(1)} collective-permute-done((bf16[1,32,3584]{2,1,0:T(8,128)(2,1)}, bf16[1,32,3584]{2,1,0:T(8,128)(2,1)S(1)}, u32[]{:S(2)}, u32[]{:S(2)}) %collective-permute-start.1) | collective-permute-done | bytes 229408 | tf_op jit(solution)/shard_map/ppermute | solution.py:13
  36.2 0.6 convolution_convert_fusion.3
  36.9 0.2 reshape.149
  37.0 2.7 broadcast_in_dim.57
  39.8 10.9 %all-to-all-start.1 = ((bf16[32,18,3584]{2,1,0:T(8,128)(2,1)}), bf16[32,18,3584]{2,1,0:T(8,128)(2,1)}, u32[]{:S(2)}, u32[]{:S(2)}) async-start(bf16[32,18,3584]{2,1,0:T(8,128)(2,1)} %bitcast.45), calls=%async_computation.1 | async-start | bytes 11010048 | tf_op jit(solution)/shard_map/all_to_all | solution.py:107
  50.8 1.9 collective-permute-start
  52.7 81.2 %collective-permute-done = bf16[1,32,3584]{2,1,0:T(8,128)(2,1)S(1)} collective-permute-done((bf16[1,32,3584]{2,1,0:T(8,128)(2,1)S(1)}, bf16[1,32,3584]{2,1,0:T(8,128)(2,1)S(1)}, u32[]{:S(2)}, u32[]{:S(2)}) %collective-permute-start) | collective-permute-done | bytes 229408 | tf_op jit(solution)/shard_map/ppermute | solution.py:13
  133.9 0.7 copy-done.2
  134.6 0.1 copy.44
  134.7 100.0 %all-gather = s32[1,1024,2]{2,0,1:T(1,128)S(1)} all-gather(s32[1,32,2]{2,0,1:T(1,128)S(1)} %copy.44), channel_id=2, replica_groups=mesh['pipe'=16,'expert'=32] {'expert'}, dimensions={1}, use_global_device_ids=true | all-gather | bytes 8448 | tf_op jit(solution)/shard_map/all_gather | solution.py:74
  234.6 0.3 copy.45
  234.9 0.5 copy.46
  235.5 0.6 fusion.30
  236.1 0.1 copy.48
  236.2 0.1 multiply_reduce_fusion
  236.3 0.1 copy.57
  236.4 0.1 copy.51
  236.5 27.2 %all-gather.4.cloned.1.call-done = bf16[1,1024,3584]{2,1,0:T(8,128)(2,1)} async-done(((bf16[1,32,3584]{2,1,0:T(8,128)(2,1)}), bf16[1,1024,3584]{2,1,0:T(8,128)(2,1)}) %all-gather.4.cloned.1.call-update) | async-done | bytes 7340048 | tf_op jit(solution)/shard_map/all_gather | solution.py:73
  263.7 7.1 %convolution_convert_fusion = bf16[32,18,3584]{2,1,0:T(8,128)(2,1)} fusion(bf16[32,32,3584]{2,1,0:T(8,128)(2,1)} %bitcast.46, s32[32,32]{1,0:T(8,128)S(1)} %copy.48, pred[32,32]{1,0:T(8,128)(4,1)S(1)} %copy.51), kind=kOutput, calls=%fused_computation.1 | convolution fusion | flops 134221824 | bytes 11473920 | tf_op jit(solution)/shard_map/nct,ntd->ncd/dot_general | solution.py:83
  270.8 7.5 %reshape.145 = bf16[576,3584]{1,0:T(8,128)(2,1)} reshape(bf16[32,18,3584]{2,1,0:T(8,128)(2,1)} %convolution_convert_fusion) | data formatting | bytes 8257536 | tf_op jit(solution)/shard_map/reshape | solution.py:48
  278.2 3.4 fusion.8
  281.6 8.6 %convolution_convert_fusion.1 = bf16[576,3584]{1,0:T(8,128)(2,1)} fusion(bf16[576,3584]{1,0:T(8,128)(2,1)} %reshape.145, bf16[1,128,3584]{2,1,0:T(8,128)(2,1)S(1)} %copy-done, bf16[1,2,3584,128]{3,2,1,0:T(8,128)(2,1)S(1)} %copy-done.1, f32[576,128]{1,0:T(8,128)S(1)} %fusion.8), kind=kOutput, calls=%fused_computation.2 | convolution fusion | flops 1059471360 | bytes 10387456 | tf_op jit(solution)/shard_map/dot_general | solution.py:52
  290.2 7.2 %reshape.146 = bf16[32,18,3584]{2,1,0:T(8,128)(2,1)} reshape(bf16[576,3584]{1,0:T(8,128)(2,1)} %convolution_convert_fusion.1) | data formatting | bytes 8257536 | tf_op jit(solution)/shard_map/reshape | solution.py:55
  297.4 6.4 %all-to-all-start = ((bf16[32,18,3584]{2,1,0:T(8,128)(2,1)}), bf16[32,18,3584]{2,1,0:T(8,128)(2,1)}, u32[]{:S(2)}, u32[]{:S(2)}) async-start(bf16[32,18,3584]{2,1,0:T(8,128)(2,1)} %reshape.146), calls=%async_computation | async-start | bytes 11010048 | tf_op jit(solution)/shard_map/all_to_all | solution.py:59
  303.9 7.4 %reshape.151 = bf16[576,3584]{1,0:T(8,128)(2,1)} reshape(bf16[32,18,3584]{2,1,0:T(8,128)(2,1)} %all-to-all-done.1) | data formatting | bytes 8257536 | tf_op jit(solution)/shard_map/reshape | solution.py:112
  311.2 3.6 fusion
  314.8 2.4 collective-permute-start.2
  317.2 21.2 %collective-permute-done.2 = bf16[128,3584]{0,1:T(8,128)(2,1)S(1)} collective-permute-done((bf16[128,3584]{0,1:T(8,128)(2,1)S(1)}, bf16[128,3584]{0,1:T(8,128)(2,1)S(1)}, u32[]{:S(2)}, u32[]{:S(2)}) %collective-permute-start.2) | collective-permute-done | bytes 917536 | tf_op jit(solution)/shard_map/ppermute | solution.py:23
  338.4 3.9 collective-permute-start.3
  342.3 20.2 %collective-permute-done.3 = bf16[128,3584]{0,1:T(8,128)(2,1)S(1)} collective-permute-done((bf16[128,3584]{0,1:T(8,128)(2,1)S(1)}, bf16[128,3584]{0,1:T(8,128)(2,1)S(1)}, u32[]{:S(2)}, u32[]{:S(2)}) %collective-permute-start.3) | collective-permute-done | bytes 917536 | tf_op jit(solution)/shard_map/ppermute | solution.py:23
  362.6 6.8 %collective-permute-start.4 = (bf16[128,3584]{0,1:T(8,128)(2,1)S(1)}, bf16[128,3584]{0,1:T(8,128)(2,1)}, u32[]{:S(2)}, u32[]{:S(2)}) collective-permute-start(bf16[128,3584]{0,1:T(8,128)(2,1)S(1)} %collective-permute-done.3), channel_id=1, source_target_pairs={{0,128},{128,0},{32,160},{160,32},{64,192},{192,64},{96,224},{224,... | collective-permute-start | bytes 2752520 | tf_op jit(solution)/shard_map/ppermute | solution.py:23
  369.4 137.7 %collective-permute-done.4 = bf16[128,3584]{0,1:T(8,128)(2,1)} collective-permute-done((bf16[128,3584]{0,1:T(8,128)(2,1)S(1)}, bf16[128,3584]{0,1:T(8,128)(2,1)}, u32[]{:S(2)}, u32[]{:S(2)}) %collective-permute-start.4) | collective-permute-done | bytes 917536 | tf_op jit(solution)/shard_map/ppermute | solution.py:23
  507.0 6.8 %collective-permute-start.5 = (bf16[128,3584]{0,1:T(8,128)(2,1)}, bf16[128,3584]{0,1:T(8,128)(2,1)}, u32[]{:S(2)}, u32[]{:S(2)}) collective-permute-start(bf16[128,3584]{0,1:T(8,128)(2,1)} %collective-permute-done.4), channel_id=1, source_target_pairs={{0,256},{256,0},{32,288},{288,32},{64,320},{320,64},{96,352},{352,... | collective-permute-start | bytes 2752520 | tf_op jit(solution)/shard_map/ppermute | solution.py:23
  513.8 0.1 copy.41
  514.0 0.1 copy.43
  514.1 0.1 fusion.27
  514.2 44.1 %collective-permute-done.5 = bf16[128,3584]{0,1:T(8,128)(2,1)} collective-permute-done((bf16[128,3584]{0,1:T(8,128)(2,1)}, bf16[128,3584]{0,1:T(8,128)(2,1)}, u32[]{:S(2)}, u32[]{:S(2)}) %collective-permute-start.5) | collective-permute-done | bytes 917536 | tf_op jit(solution)/shard_map/ppermute | solution.py:23
  558.4 1.4 fusion.4
  559.8 1.3 copy.56
  561.1 3.6 convert_reduce_fusion
  564.7 2.1 fusion.2
  (26 shorter events, 0.3 us)
Async XLA Ops:
  7.2 274.5 %copy-start = (bf16[1,128,3584]{2,1,0:T(8,128)(2,1)S(1)}, bf16[1,128,3584]{2,1,0:T(8,128)(2,1)}, u32[]{:S(2)}) copy-start(bf16[1,128,3584]{2,1,0:T(8,128)(2,1)} %param.16) | copy-start | bytes 2752516
  7.2 29.1 %collective-permute-start.1 = (bf16[1,32,3584]{2,1,0:T(8,128)(2,1)}, bf16[1,32,3584]{2,1,0:T(8,128)(2,1)S(1)}, u32[]{:S(2)}, u32[]{:S(2)}) collective-permute-start(bf16[1,32,3584]{2,1,0:T(8,128)(2,1)} %param.10), channel_id=1, source_target_pairs={{0,480},{32,0},{64,32},{96,64},{128,96},{160,128},{192,160},{224,1... | collective-permute-start | bytes 688136 | tf_op jit(solution)/shard_map/ppermute | solution.py:13
  39.8 11.0 %copy-start.6 = (bf16[1,32,3584]{2,1,0:T(8,128)(2,1)S(1)}, bf16[1,32,3584]{2,1,0:T(8,128)(2,1)}, u32[]{:S(2)}) copy-start(bf16[1,32,3584]{2,1,0:T(8,128)(2,1)} %param.9) | copy-start | bytes 688132
  39.8 94.8 %copy-start.4 = (s32[1,32,2]{1,2,0:T(2,128)S(1)}, s32[1,32,2]{1,2,0:T(2,128)}, u32[]{:S(2)}) copy-start(s32[1,32,2]{1,2,0:T(2,128)} %param.11) | copy-start | bytes 772
  39.8 257.7 %all-to-all-start.1 = ((bf16[32,18,3584]{2,1,0:T(8,128)(2,1)}), bf16[32,18,3584]{2,1,0:T(8,128)(2,1)}, u32[]{:S(2)}, u32[]{:S(2)}) async-start(bf16[32,18,3584]{2,1,0:T(8,128)(2,1)} %bitcast.45), calls=%async_computation.1 | async-start | bytes 11010048 | tf_op jit(solution)/shard_map/all_to_all | solution.py:107
  50.7 213.0 %all-gather.4.cloned.1.call-start = ((), (), s32[]{:S(2)}) async-start(), calls=%async_computation.2 | async-start | bytes 7569408 | tf_op jit(solution)/shard_map/all_gather | solution.py:73
  50.8 83.1 %collective-permute-start = (bf16[1,32,3584]{2,1,0:T(8,128)(2,1)S(1)}, bf16[1,32,3584]{2,1,0:T(8,128)(2,1)S(1)}, u32[]{:S(2)}, u32[]{:S(2)}) collective-permute-start(bf16[1,32,3584]{2,1,0:T(8,128)(2,1)S(1)} %copy-done.6), channel_id=1, source_target_pairs={{0,32},{32,64},{64,96},{96,128},{128,160},{160,192},{192,224},{224... | collective-permute-start | bytes 688136 | tf_op jit(solution)/shard_map/ppermute | solution.py:13
  133.9 0.7 copy-start.2
  270.8 7.5 %copy-start.1 = (bf16[1,2,3584,128]{3,2,1,0:T(8,128)(2,1)S(1)}, bf16[1,2,3584,128]{3,2,1,0:T(8,128)(2,1)}, u32[]{:S(2)}) copy-start(bf16[1,2,3584,128]{3,2,1,0:T(8,128)(2,1)} %param.15) | copy-start | bytes 5505028
  297.4 263.6 %all-to-all-start = ((bf16[32,18,3584]{2,1,0:T(8,128)(2,1)}), bf16[32,18,3584]{2,1,0:T(8,128)(2,1)}, u32[]{:S(2)}, u32[]{:S(2)}) async-start(bf16[32,18,3584]{2,1,0:T(8,128)(2,1)} %reshape.146), calls=%async_computation | async-start | bytes 11010048 | tf_op jit(solution)/shard_map/all_to_all | solution.py:59
  303.8 7.4 %copy-start.3 = (bf16[1,576,128]{2,1,0:T(8,128)(2,1)S(1)}, bf16[1,576,128]{2,1,0:T(8,128)(2,1)}, u32[]{:S(2)}) copy-start(bf16[1,576,128]{2,1,0:T(8,128)(2,1)} %param.17) | copy-start | bytes 442372
  311.2 202.8 %copy-start.5 = (f32[1,32,2]{1,2,0:T(2,128)S(1)}, f32[1,32,2]{1,2,0:T(2,128)}, u32[]{:S(2)}) copy-start(f32[1,32,2]{1,2,0:T(2,128)} %param.12) | copy-start | bytes 772
  314.8 23.6 %collective-permute-start.2 = (bf16[128,3584]{0,1:T(8,128)(2,1)S(1)}, bf16[128,3584]{0,1:T(8,128)(2,1)S(1)}, u32[]{:S(2)}, u32[]{:S(2)}) collective-permute-start(bf16[128,3584]{0,1:T(8,128)(2,1)S(1)} %fusion), channel_id=1, source_target_pairs={{0,32},{32,0},{64,96},{96,64},{128,160},{160,128},{192,224},{224,1... | collective-permute-start | bytes 2752520 | tf_op jit(solution)/shard_map/ppermute | solution.py:23
  338.4 24.1 %collective-permute-start.3 = (bf16[128,3584]{0,1:T(8,128)(2,1)S(1)}, bf16[128,3584]{0,1:T(8,128)(2,1)S(1)}, u32[]{:S(2)}, u32[]{:S(2)}) collective-permute-start(bf16[128,3584]{0,1:T(8,128)(2,1)S(1)} %collective-permute-done.2), channel_id=1, source_target_pairs={{0,64},{64,0},{32,96},{96,32},{128,192},{192,128},{160,224},{224,1... | collective-permute-start | bytes 2752520 | tf_op jit(solution)/shard_map/ppermute | solution.py:23
  362.6 144.5 %collective-permute-start.4 = (bf16[128,3584]{0,1:T(8,128)(2,1)S(1)}, bf16[128,3584]{0,1:T(8,128)(2,1)}, u32[]{:S(2)}, u32[]{:S(2)}) collective-permute-start(bf16[128,3584]{0,1:T(8,128)(2,1)S(1)} %collective-permute-done.3), channel_id=1, source_target_pairs={{0,128},{128,0},{32,160},{160,32},{64,192},{192,64},{96,224},{224,... | collective-permute-start | bytes 2752520 | tf_op jit(solution)/shard_map/ppermute | solution.py:23
  507.0 51.3 %collective-permute-start.5 = (bf16[128,3584]{0,1:T(8,128)(2,1)}, bf16[128,3584]{0,1:T(8,128)(2,1)}, u32[]{:S(2)}, u32[]{:S(2)}) collective-permute-start(bf16[128,3584]{0,1:T(8,128)(2,1)} %collective-permute-done.4), channel_id=1, source_target_pairs={{0,256},{256,0},{32,288},{288,32},{64,320},{320,64},{96,352},{352,... | collective-permute-start | bytes 2752520 | tf_op jit(solution)/shard_map/ppermute | solution.py:23
Sparse Core Ops, SparseCore 0:
  134.7 128.9 all-gather.3
where the time goes:
time: 575 us; the launch traced here: 574 us
  waiting for transfers between devices  346 us (60%)
  blocking collectives  100 us (17%)
  starting transfers between devices  52.4 us (9%)
  local copies, waits for them, and re-layouts  28.5 us (5%)
  matrix products  25.3 us (4%)
  between operations  14.3 us (2%)
  other arithmetic  7.55 us (1%)
    ppermute x4, waiting for transfers between devices, swapped(): return lax.ppermute(block, axis, route)  223 us
    all_gather x1, blocking collectives, shards(): piece_routes = lax.all_gather(routes_here, 'expert', axis=0, tiled=True)  100 us
    ppermute x2, waiting for transfers between devices, passed_along(): return lax.ppermute(value, axis, pairs)  95.1 us
    all_gather x1, waiting for transfers between devices, shards(): token_rows = lax.all_gather(tokens, 'expert', axis=0, tiled=True)  27.2 us
    ppermute x4, starting transfers between devices, swapped(): return lax.ppermute(block, axis, route)  19.9 us
    ppermute x2, starting transfers between devices, passed_along(): return lax.ppermute(value, axis, pairs)  15.2 us
  transfers between devices with their start and end apart: 9, of which 7 were waited for; matrix products, arithmetic and copies ran while one was open for 9% of the time, Pallas kernels for 0%

commit v1 on v0

v1 whole, which is shorter than its diff:
```python
import jax
import jax.numpy as jnp
from jax import lax
from jax.experimental import pallas as pl
from jax.experimental.pallas import tpu as pltpu
from jax.sharding import PartitionSpec as P

MESH = pl.DeviceIdType.MESH
EXPERTS = 4
CAP = 18
TOK = 32
D = 3584
HALF = 1792
QUART = 896
HID = 128
SLOTS = 576
BLOCK = 144
WIDE = 512
F32 = jnp.float32
BF16 = jnp.bfloat16


def iota(shape, axis):
    return lax.broadcasted_iota(jnp.int32, shape, axis)


def piece_width(k):
    return min(WIDE, HALF - k * WIDE)


def kernel(
    meta_ref, act_ref, cot_ref, win_ref, wdn_ref, stash_ref,
    moe_ref, grad_ref,
    meta_p, meta_c, meta_m,
    hop_f, hop_b, hop_m,
    sa_f, sa_b, sa_m, sl_f, sl_b, sl_m,
    lr_f, lr_b, lr_m, lr_r,
    x_f, x_b, x_m,
    win, wd, st, stm, sp32, spt, spmt,
    pre, pre_r, hid,
    po32, po, r_opp_l, r_opp_r, acc_r, acc_l, r_l, r_r,
    ret, ret_l, rows_r, mo, own_g, g,
    send_sem, recv_sem, local_sem,
):
    p = lax.axis_index("pipe")
    i = lax.axis_index("expert")
    n_pipe = lax.axis_size("pipe")
    c = lax.rem(i, 2)
    xq = lax.rem(lax.div(i, 2), 4)
    l = lax.div(i, 8)

    def at(pp, ll, xx, cc):
        return (pp, ll * 8 + xx * 2 + cc)

    nxt = lax.rem(p + 1, n_pipe)
    prv = lax.rem(p + n_pipe - 1, n_pipe)
    mirror = at(n_pipe - 1 - p, l, xq, c)
    partner = at(p, l, xq, 1 - c)
    right = at(p, l, lax.rem(xq + 1, 4), c)
    left = at(p, l, lax.rem(xq + 3, 4), c)

    def zdev(d):
        return lax.rem(l + d, 4)

    barrier = pltpu.get_barrier_semaphore()
    greeted = [at(q, l, xq, cc) for q in (nxt, prv) for cc in (c, 1 - c)]
    greeted += [at(p, zdev(d), xq, c) for d in (1, 2, 3)]
    greeted += [mirror, partner, right, left]
    for other in greeted:
        pl.semaphore_signal(barrier, inc=1, device_id=other, device_id_type=MESH)
    pl.semaphore_wait(barrier, len(greeted))

    used = [0, 0]
    sent = []
    local = []

    def remote(src, dst, device):
        k = used[0]
        used[0] += 1
        copy = pltpu.make_async_remote_copy(
            src_ref=src, dst_ref=dst, send_sem=send_sem.at[k], recv_sem=recv_sem.at[k],
            device_id=device, device_id_type=MESH,
        )
        copy.start()
        sent.append(copy)
        return copy

    def here(src, dst):
        k = used[1]
        used[1] += 1
        copy = pltpu.make_async_copy(src, dst, local_sem.at[k])
        copy.start()
        return copy

    def half_of(core):
        return pl.ds(pl.multiple_of(core * HALF, HALF), HALF)

    mine = pl.ds(pl.multiple_of(c * TOK, TOK), TOK)
    hops_f = []
    hops_b = []
    for d in (0, 1):
        core = lax.rem(c + d, 2)
        hops_f.append(remote(act_ref.at[0, :, half_of(core)], hop_f.at[mine], at(nxt, l, xq, core)))
        hops_b.append(remote(cot_ref.at[0, :, half_of(core)], hop_b.at[mine], at(prv, l, xq, core)))
    meta_copy = remote(meta_ref, meta_p, partner)
    stash_own = here(stash_ref.at[0], st.at[:, 0:HID])
    stash_other = remote(stash_ref.at[0], st.at[:, HID:2 * HID], partner)
    weights = []
    weights_other = []
    for s in (0, 1):
        weights.append(here(win_ref.at[0, s, half_of(c)], win.at[:, s * HID:(s + 1) * HID]))
        weights_other.append(
            remote(win_ref.at[0, s, half_of(1 - c)], win.at[:, (2 + s) * HID:(3 + s) * HID], partner)
        )
    weights.append(here(wdn_ref.at[0, :, half_of(c)], wd.at[0:HID]))
    weights_other.append(remote(wdn_ref.at[0, :, half_of(1 - c)], wd.at[HID:2 * HID], partner))

    meta_copy.wait_recv()
    meta_c[...] = meta_ref[...] + meta_p[...]

    def first_slots(meta, row):
        j = iota((32, 64), 0)
        lane = iota((32, 64), 1)
        core = (j >= CAP).astype(jnp.int32)
        wanted = (j - CAP * core + 1).astype(F32)
        same = (lane >= TOK).astype(jnp.int32) == core
        return [
            jnp.where((meta[row + e:row + e + 1, 0:64] == wanted) & same, 1.0, 0.0).astype(F32)
            for e in range(EXPERTS)
        ]

    def last_slots(meta, row, rows):
        r = iota((rows, 64), 0)
        lane = iota((rows, 64), 1)
        wanted = ((r & 3) + (32 - CAP + 1)).astype(F32)
        return [
            jnp.where((meta[row + e:row + e + 1, 0:64] == wanted) & (lane >= TOK), 1.0, 0.0).astype(F32)
            for e in range(EXPERTS)
        ]

    def chosen_rows(meta, row, weigh, hop, sa, sl):
        a = first_slots(meta, row)
        b = last_slots(meta, row, 16)
        sel_a = jnp.concatenate(a, axis=0)
        sel_b = jnp.concatenate(b, axis=0)
        if weigh:
            gates = [meta[row + 4 + e:row + 5 + e, 0:64] for e in range(EXPERTS)]
            gate_a = jnp.sum(jnp.concatenate([v * w for v, w in zip(a, gates)], axis=0), axis=1, keepdims=True)
            gate_b = jnp.sum(jnp.concatenate([v * w for v, w in zip(b, gates)], axis=0), axis=1, keepdims=True)
        sel_a = sel_a.astype(BF16)
        for t in range(7):
            cols = slice(t * 256, (t + 1) * 256)
            got = jnp.dot(sel_a, hop[:, cols], preferred_element_type=F32)
            if weigh:
                got = got * gate_a
            sa[:, cols] = got.astype(BF16)
        piece = (iota((64, 64), 0) >> 2) & 3
        parts = [jnp.where(piece == k, sel_b, 0.0).astype(BF16) for k in range(4)]
        for t in range(2):
            total = None
            for k in range(4):
                if t * 256 < piece_width(k):
                    low = k * WIDE + t * 256
                    got = jnp.dot(parts[k], hop[:, low:low + 256], preferred_element_type=F32)
                    total = got if total is None else total + got
            if weigh:
                total = total * gate_b
            sl[:, t * 256:(t + 1) * 256] = total.astype(BF16)

    rows_here = pl.ds(pl.multiple_of(l * 32, 32), 32)
    last_here = pl.ds(pl.multiple_of(l * 16, 16), 16)

    def exchange(sa, sl, rows, last):
        out = []
        for d in (2, 1, 3):
            e = zdev(d)
            device = at(p, e, xq, c)
            out.append(remote(sa.at[pl.ds(pl.multiple_of(e * 32, 32), 32)], rows.at[rows_here], device))
            out.append(remote(sl.at[pl.ds(pl.multiple_of(e * 16, 16), 16)], last.at[last_here], device))
        own = [here(sa.at[rows_here], rows.at[rows_here]), here(sl.at[last_here], last.at[last_here])]
        return out, own

    def arrived(copies):
        for copy in copies[0]:
            copy.wait_recv()
        for copy in copies[1]:
            copy.wait()

    def spread_last(last, rows):
        m = iota((16, 64), 0)
        n = iota((16, 64), 1)
        for k in range(4):
            width = piece_width(k)
            place = (m >> 2) * 16 + 4 * k + (m & 3)
            pick = jnp.where(n == place, 1.0, 0.0).astype(BF16)
            got = jnp.dot(pick, last[:, 0:width], preferred_element_type=F32)
            rows[128:BLOCK, k * WIDE:k * WIDE + width] = got.astype(BF16)

    def block(k):
        return slice(k * BLOCK, (k + 1) * BLOCK)

    A = slice(0, QUART)
    B = slice(QUART, HALF)

    def gather_start(x):
        ra = remote(x.at[block(0), A], x.at[block(1), A], right)
        lb = remote(x.at[block(0), B], x.at[block(2), B], left)
        rb = remote(x.at[block(0), B], x.at[block(1), B], right)
        la = remote(x.at[block(0), A], x.at[block(2), A], left)
        return [ra, lb, rb, la]

    def gather_forward(x, copies):
        copies[0].wait_recv()
        fr = remote(x.at[block(1), A], x.at[block(3), A], right)
        copies[1].wait_recv()
        fl = remote(x.at[block(2), B], x.at[block(3), B], left)
        return copies + [fr, fl]

    def permuted(source, target):
        for k, step in enumerate((0, 3, 1, 2)):
            m = iota((BLOCK, SLOTS), 0)
            n = iota((BLOCK, SLOTS), 1)
            at_x = lax.rem(xq + step, 4)
            early = (m >> 5) * BLOCK + (m & 31)
            late = ((m - 128) >> 2) * BLOCK + 32 + (m & 3)
            origin = jnp.where(m < 128, early, late) + at_x * 36
            pick = jnp.where(n == origin, 1.0, 0.0).astype(BF16)
            sp32[block(k)] = jnp.dot(pick, source[...], preferred_element_type=F32)
        target[...] = sp32[...].T.astype(BF16)

    stash_own.wait()
    stash_other.wait_recv()
    permuted(st, spt)

    for copy in hops_f:
        copy.wait_recv()
    chosen_rows(meta_c, 0, False, hop_f, sa_f, sl_f)
    to_f = exchange(sa_f, sl_f, x_f, lr_f)
    for copy in hops_b:
        copy.wait_recv()
    mirror_meta = remote(meta_c, meta_m, mirror)
    mirror_rows = remote(hop_b, hop_m, mirror)
    mirror_stash = remote(stash_ref.at[0], stm.at[:, 0:HID], mirror)
    chosen_rows(meta_c, 8, True, hop_b, sa_b, sl_b)
    to_b = exchange(sa_b, sl_b, x_b, lr_b)

    arrived(to_f)
    spread_last(lr_f, x_f)
    ag_f = gather_start(x_f)

    for copy in weights:
        copy.wait()
    for copy in weights_other:
        copy.wait_recv()

    def project(k):
        pre[block(k)] = jnp.dot(x_f[block(k)], win[...], preferred_element_type=F32)
        return remote(pre.at[block(k), 2 * HID:4 * HID], pre_r.at[block(k)], partner)

    def activate(k, copy):
        copy.wait_recv()
        gate = pre[block(k), 0:HID] + pre_r[block(k), 0:HID]
        up = pre[block(k), HID:2 * HID] + pre_r[block(k), HID:2 * HID]
        hid[block(k), 0:HID] = (gate / (1.0 + jnp.exp(-gate)) * up).astype(BF16)
        return remote(hid.at[block(k), 0:HID], hid.at[block(k), HID:2 * HID], partner)

    def down(k, copy):
        copy.wait_recv()

        @pl.loop(0, 7)
        def _(t):
            cols = pl.ds(pl.multiple_of(t * 256, 256), 256)
            got = jnp.dot(hid[block(k)], wd[:, cols], preferred_element_type=F32)
            po32[block(k), cols] = got
            po[block(k), cols] = got.astype(BF16)

    pre_0 = project(0)
    arrived(to_b)
    spread_last(lr_b, x_b)
    hid_0 = activate(0, pre_0)

    ag_f = gather_forward(x_f, ag_f)
    ag_b = gather_start(x_b)
    ag_f[2].wait_recv()
    ag_f[3].wait_recv()
    pre_1 = project(1)
    pre_2 = project(2)
    hid_1 = activate(1, pre_1)
    hid_2 = activate(2, pre_2)
    down(1, hid_1)
    to_left_a = remote(po.at[block(1), A], r_r.at[:, A], left)
    down(2, hid_2)
    to_right_b = remote(po.at[block(2), B], r_l.at[:, B], right)
    ag_f[4].wait_recv()
    ag_f[5].wait_recv()
    pre_3 = project(3)
    hid_3 = activate(3, pre_3)
    down(3, hid_3)
    opp_a = remote(po.at[block(3), A], r_opp_l, right)
    opp_b = remote(po.at[block(3), B], r_opp_r, left)
    down(0, hid_0)
    ag_b = gather_forward(x_b, ag_b)

    mirror_meta.wait_recv()
    mirror_rows.wait_recv()
    chosen_rows(meta_m, 8, True, hop_m, sa_m, sl_m)
    to_m = exchange(sa_m, sl_m, x_m, lr_m)
    mirror_stash.wait_recv()
    stash_pass = remote(stm.at[:, 0:HID], stm.at[:, HID:2 * HID], partner)

    opp_a.wait_recv()
    acc_r[...] = (po32[block(2), A] + r_opp_l[...].astype(F32)).astype(BF16)
    to_right_a = remote(acc_r, r_l.at[:, A], right)
    opp_b.wait_recv()
    acc_l[...] = (po32[block(1), B] + r_opp_r[...].astype(F32)).astype(BF16)
    to_left_b = remote(acc_l, r_r.at[:, B], left)

    arrived(to_m)
    spread_last(lr_m, x_m)
    ag_m = gather_start(x_m)

    stash_pass.wait_recv()
    permuted(stm, spmt)

    for copy in (to_right_a, to_right_b, to_left_a, to_left_b):
        copy.wait_recv()
    ret[...] = (po32[block(0)] + r_l[...].astype(F32) + r_r[...].astype(F32)).astype(BF16)
    m = iota((64, 16), 0)
    n = iota((64, 16), 1)
    place = (m >> 4) * 4 + (m & 3)
    for t in range(2):
        total = None
        for k in range(4):
            if t * 256 < piece_width(k):
                pick = jnp.where((n == place) & (((m >> 2) & 3) == k), 1.0, 0.0).astype(BF16)
                low = k * WIDE + t * 256
                got = jnp.dot(pick, ret[128:BLOCK, low:low + 256], preferred_element_type=F32)
                total = got if total is None else total + got
        ret_l[:, t * 256:(t + 1) * 256] = total.astype(BF16)
    to_r = exchange(ret, ret_l, rows_r, lr_r)

    ag_m = gather_forward(x_m, ag_m)
    for copy in ag_b[2:]:
        copy.wait_recv()

    @pl.loop(0, 7)
    def _(t):
        cols = pl.ds(pl.multiple_of(t * 256, 256), 256)
        own_g[:, cols] = jnp.dot(spt[...], x_b[:, cols], preferred_element_type=F32).astype(BF16)

    gates = [meta_c[4 + e:5 + e, 0:64] for e in range(EXPERTS)]
    table = [v * w for v, w in zip(first_slots(meta_c, 0), gates)]
    late = last_slots(meta_c, 0, 16)
    row = iota((16, 64), 0) >> 2
    tail = None
    for e in range(EXPERTS):
        part = jnp.where(row == e, late[e] * gates[e], 0.0)
        tail = part if tail is None else tail + part
    table = jnp.concatenate(table + [tail], axis=0).T
    table_hi = table.astype(BF16)
    table_lo = (table - table_hi.astype(F32)).astype(BF16)
    arrived(to_r)
    spread_last(lr_r, rows_r)
    for t in range(7):
        cols = slice(t * 256, (t + 1) * 256)
        got = jnp.dot(table_hi, rows_r[:, cols], preferred_element_type=F32)
        got += jnp.dot(table_lo, rows_r[:, cols], preferred_element_type=F32)
        mo[:, cols] = got.astype(BF16)
    theirs = pl.ds(pl.multiple_of((1 - c) * TOK, TOK), TOK)
    moe_other = remote(mo.at[theirs], moe_ref.at[0, :, half_of(c)], partner)
    moe_own = here(mo.at[mine], moe_ref.at[0, :, half_of(c)])

    for copy in ag_m[2:]:
        copy.wait_recv()

    @pl.loop(0, 7)
    def _(t):
        cols = pl.ds(pl.multiple_of(t * 256, 256), 256)
        other = jnp.dot(spmt[...], x_m[:, cols], preferred_element_type=F32).astype(BF16)
        g[:, cols] = (own_g[:, cols].astype(F32) + other.astype(F32)).astype(BF16)

    grad_other = remote(g.at[HID:2 * HID], grad_ref.at[0, :, half_of(c)], partner)
    grad_own = here(g.at[0:HID], grad_ref.at[0, :, half_of(c)])

    moe_own.wait()
    grad_own.wait()
    moe_other.wait_recv()
    grad_other.wait_recv()
    for copy in sent:
        copy.wait_send()


def slot_meta(routes, gates, core):
    ids = jnp.arange(EXPERTS, dtype=jnp.int32)
    match = routes[:, :, None] == ids
    hits = jnp.any(match, axis=1).astype(F32)
    weight = jnp.sum(jnp.where(match, gates[:, :, None], 0.0), axis=1)
    t = jnp.arange(TOK, dtype=jnp.int32)
    upto = (t[:, None] >= t[None, :]).astype(F32)
    count = jnp.sum(upto[:, :, None] * hits[None], axis=1)
    both = jnp.concatenate([(count * hits).T, weight.T], axis=0)
    lane_core = jnp.arange(128, dtype=jnp.int32) // TOK
    return jnp.where(lane_core[None, :] == core, jnp.tile(both, (1, 4)), 0.0)


def shards(act_fwd, cot_bwd, routes_fwd, gates_fwd, routes_bwd, gates_bwd, w_in, w_down, stash):
    core = lax.axis_index("expert") % 2
    meta = jnp.concatenate(
        [slot_meta(routes_fwd[0], gates_fwd[0], core), slot_meta(routes_bwd[0], gates_bwd[0], core)],
        axis=0,
    )
    V = pltpu.VMEM
    scratch = [
        V((16, 128), F32), V((16, 128), F32), V((16, 128), F32),
        V((64, HALF), BF16), V((64, HALF), BF16), V((64, HALF), BF16),
        V((128, HALF), BF16), V((128, HALF), BF16), V((128, HALF), BF16),
        V((64, WIDE), BF16), V((64, WIDE), BF16), V((64, WIDE), BF16),
        V((64, WIDE), BF16), V((64, WIDE), BF16), V((64, WIDE), BF16), V((64, WIDE), BF16),
        V((SLOTS, HALF), BF16), V((SLOTS, HALF), BF16), V((SLOTS, HALF), BF16),
        V((HALF, 4 * HID), BF16), V((2 * HID, HALF), BF16),
        V((SLOTS, 2 * HID), BF16), V((SLOTS, 2 * HID), BF16),
        V((SLOTS, 2 * HID), F32), V((2 * HID, SLOTS), BF16), V((2 * HID, SLOTS), BF16),
        V((SLOTS, 4 * HID), F32), V((SLOTS, 2 * HID), F32), V((SLOTS, 2 * HID), BF16),
        V((SLOTS, HALF), F32), V((SLOTS, HALF), BF16),
        V((BLOCK, QUART), BF16), V((BLOCK, QUART), BF16), V((BLOCK, QUART), BF16), V((BLOCK, QUART), BF16),
        V((BLOCK, HALF), BF16), V((BLOCK, HALF), BF16),
        V((BLOCK, HALF), BF16), V((64, WIDE), BF16), V((BLOCK, HALF), BF16),
        V((64, HALF), BF16), V((2 * HID, HALF), BF16), V((2 * HID, HALF), BF16),
        pltpu.SemaphoreType.DMA((80,)), pltpu.SemaphoreType.DMA((80,)), pltpu.SemaphoreType.DMA((24,)),
    ]
    anywhere = pl.BlockSpec(memory_space=pl.ANY)
    return pl.pallas_call(
        kernel,
        out_shape=(
            jax.ShapeDtypeStruct((1, TOK, D), BF16),
            jax.ShapeDtypeStruct((1, HID, D), BF16),
        ),
        in_specs=[pl.BlockSpec(memory_space=pltpu.VMEM)] + [anywhere] * 5,
        out_specs=(anywhere, anywhere),
        scratch_shapes=scratch,
        compiler_params=pltpu.CompilerParams(
            collective_id=0, has_side_effects=True, vmem_limit_bytes=50 * 1024 * 1024
        ),
    )(meta, act_fwd, cot_bwd, w_in, w_down, stash)


def solution(mesh):
    rows = P("pipe", "expert", None)
    in_specs = (rows, rows, rows, rows, rows, rows, P("pipe", None, None, "expert"), rows, rows)
    return jax.shard_map(shards, mesh=mesh, in_specs=in_specs, out_specs=(rows, rows), check_vma=False)
```

time: 575 us -> 154 us (0.27)
  the two profiles are of different devices: /device:TPU:65 before, /device:TPU:35 now
where the time goes in v1:
time: 154 us
  Pallas kernels  145 us (94%)
  local copies, waits for them, and re-layouts  5.75 us (4%)
  other arithmetic  2.98 us (2%)
    pallas_call x1, Pallas kernels, shards(): pl.pallas_call(kernel, out_shape=(jax.ShapeDtypeStruct((1, TOK, D), BF16)...  145 us
    unnamed x10, local copies, waits for them, and re-layouts  5.58 us

profile of v1, /device:TPU:35, one launch (start us, length us, event | category | flops | bytes accessed | tf_op | source)
XLA Modules:
  0.0 154.1 jit_solution(5868107553421551484)
XLA Ops:
  0.7 0.7 fusion.2
  1.3 0.7 fusion.1
  2.1 0.7 select_reduce_fusion.1
  2.8 0.7 select_reduce_fusion
  3.5 0.1 multiply_reduce_fusion.1
  3.7 0.1 tile.9
  3.7 0.1 tile.21
  3.8 0.0 copy-start
  3.8 1.2 copy-done
  5.0 0.0 copy-start.1
  5.0 0.9 copy-done.1
  6.0 0.0 copy-start.2
  6.0 0.9 copy-done.2
  6.9 0.0 copy-start.3
  6.9 0.9 copy-done.3
  7.8 144.7 %shard_map.104 = (bf16[1,32,3584]{2,1,0:T(8,128)(2,1)S(1)}, bf16[1,128,3584]{2,1,0:T(8,128)(2,1)S(1)}) custom-call(f32[16,128]{1,0:T(8,128)S(1)} %pad_maximum_fusion.meta_ref, bf16[1,32,3584]{2,1,0:T(8,128)(2,1)S(1)} %copy-done.1, bf16[1,32,3584]{2,1,0:T(8,128)(2,1)S(1)} %copy-done.2, bf16[1,2,3584,128]{3,2,1,0:T(8,128)(2,1)} %win_ref.1, ...), custom_call_target="tpu_custom_call" | custom-call | tf_op jit(solution)/shard_map/pallas_call | solution.py:432
  152.5 0.7 copy.19
  153.2 0.9 copy.20
  (11 shorter events, 0.1 us)
Async XLA Ops:
  3.8 1.2 copy-start
  5.0 0.9 copy-start.1
  6.0 0.9 copy-start.2
  6.9 0.9 copy-start.3

commit v2 on v1

v2 whole, which is shorter than its diff:
```python
import jax
import jax.numpy as jnp
from jax import lax
from jax.experimental import pallas as pl
from jax.experimental.pallas import tpu as pltpu
from jax.sharding import PartitionSpec as P

MESH = pl.DeviceIdType.MESH
EXPERTS = 4
CAP = 18
TOK = 32
D = 3584
HALF = 1792
QUART = 896
HID = 128
SLOTS = 576
BLOCK = 144
PIECE = 256
F32 = jnp.float32
BF16 = jnp.bfloat16


def iota(shape, axis):
    return lax.broadcasted_iota(jnp.int32, shape, axis)


def piece_width(k):
    return min(PIECE, QUART - k * PIECE)


def kernel(
    route_f_ref, gate_f_ref, route_b_ref, gate_b_ref, act_ref, cot_ref, win_ref, wdn_ref, stash_ref,
    moe_ref, grad_ref,
    meta_o, meta_p, meta_c, meta_m,
    hop_f, hop_b, hop_m, via_f1, via_f2, via_b1, via_b2,
    sa_f, sa_b, sa_m, sl_f, sl_b, sl_m,
    lr_f, lr_b, lr_m, lr_r,
    x_f, x_b, x_m,
    win, wd, st, stm, sp32, spt, spmt,
    pre, pre_r, hid,
    po32, po, r_opp_l, r_opp_r, acc_r, acc_l, r_l, r_r,
    ret, ret_l, rows_r, mo, own_g, g,
    send_sem, recv_sem, local_sem, hop_send, hop_recv,
):
    p = lax.axis_index("pipe")
    i = lax.axis_index("expert")
    n_pipe = lax.axis_size("pipe")
    c = lax.rem(i, 2)
    xq = lax.rem(lax.div(i, 2), 4)
    l = lax.div(i, 8)

    def at(pp, ll, xx, cc):
        return (pp, ll * 8 + xx * 2 + cc)

    y = lax.rem(p, 4)
    zh = lax.div(p, 4)
    n_zh = n_pipe // 4

    def section(yy, up):
        return lax.rem(zh + n_zh + up, n_zh) * 4 + yy

    mirror = at(n_pipe - 1 - p, l, xq, c)
    partner = at(p, l, xq, 1 - c)
    right = at(p, l, lax.rem(xq + 1, 4), c)
    left = at(p, l, lax.rem(xq + 3, 4), c)

    def zdev(d):
        return lax.rem(l + d, 4)

    barrier = pltpu.get_barrier_semaphore()
    greeted = [at(section(lax.rem(y + d, 4), 0), l, xq, cc) for d in (1, 2, 3) for cc in (c, 1 - c)]
    greeted += [at(section(y, up), l, xq, cc) for up in (1, -1) for cc in (c, 1 - c)]
    greeted += [at(p, zdev(d), xq, c) for d in (1, 2, 3)]
    greeted += [mirror, partner, right, left]
    for other in greeted:
        pl.semaphore_signal(barrier, inc=1, device_id=other, device_id_type=MESH)

    used = [0, 0]
    sent = []

    def remote(src, dst, device):
        k = used[0]
        used[0] += 1
        copy = pltpu.make_async_remote_copy(
            src_ref=src, dst_ref=dst, send_sem=send_sem.at[k], recv_sem=recv_sem.at[k],
            device_id=device, device_id_type=MESH,
        )
        copy.start()
        sent.append(copy)
        return copy

    def here(src, dst):
        k = used[1]
        used[1] += 1
        copy = pltpu.make_async_copy(src, dst, local_sem.at[k])
        copy.start()
        return copy

    def half_of(core):
        return pl.ds(pl.multiple_of(core * HALF, HALF), HALF)

    def quarter_of(core, q):
        return pl.ds(pl.multiple_of(core * HALF + q * QUART, 128), QUART)

    def cols_of(q):
        return slice(q * QUART, (q + 1) * QUART)

    A = cols_of(0)
    B = cols_of(1)
    mine = pl.ds(pl.multiple_of(c * TOK, TOK), TOK)

    def table_rows(routes, gates, row):
        e = iota((8, TOK), 0)
        first = routes[0:1] == e
        second = routes[1:2] == e
        hits = jnp.where(first | second, 1.0, 0.0).astype(F32)
        weight = jnp.where(first, gates[0:1], 0.0) + jnp.where(second, gates[1:2], 0.0)
        t = iota((TOK, 128), 0)
        lane = iota((TOK, 128), 1) - c * TOK
        upto = jnp.where((t <= lane) & (lane < TOK), 1.0, 0.0).astype(F32)
        place = jnp.where(t == lane, 1.0, 0.0).astype(F32)
        count = jnp.dot(hits, upto, preferred_element_type=F32)
        placed = jnp.dot(hits, place, preferred_element_type=F32)
        meta_o[row:row + 8] = count * placed
        meta_o[row + 8:row + 16] = jnp.dot(
            weight, place, precision=lax.Precision.HIGHEST, preferred_element_type=F32
        )

    table_rows(route_f_ref, gate_f_ref, 0)
    table_rows(route_b_ref, gate_b_ref, 16)
    weights = []
    for s in (0, 1):
        weights.append(here(win_ref.at[0, s, half_of(c)], win.at[:, s * HID:(s + 1) * HID]))
    weights.append(here(wdn_ref.at[0, :, half_of(c)], wd.at[0:HID]))
    stash_own = here(stash_ref.at[0], st.at[:, 0:HID])

    pl.semaphore_wait(barrier, len(greeted))

    def hop(k, src, dst, device, base):
        return pltpu.make_async_remote_copy(
            src_ref=src, dst_ref=dst, send_sem=hop_send.at[base + k], recv_sem=hop_recv.at[base + k],
            device_id=device, device_id_type=MESH,
        )

    class Stream:
        def __init__(self, src, rows, via_1, via_2, base, first, up, column):
            self.src, self.rows, self.via_1, self.via_2, self.base = src, rows, via_1, via_2, base
            self.up, self.column, self.ahead = up, column, up
            self.first = first
            self.last = 3 - first
            self.at_first = y == first
            self.at_last = y == self.last

        def piece(self, k):
            return self.src.at[0, :, pl.ds(pl.multiple_of(k * QUART, 128), QUART)]

        def final(self, src, core, q, device):
            cols = pl.ds(pl.multiple_of(q * QUART, 128), QUART)
            return hop(2 * q + lax.rem(c + core, 2), src, self.rows.at[mine, cols], device, self.base)

        def start(self):
            @pl.when(jnp.logical_not(self.at_last))
            def _():
                for q in (0, 1):
                    for d in (0, 1):
                        core = lax.rem(c + d, 2)
                        device = at(section(y + self.ahead, 0), l, xq, core)
                        self.final(self.piece(2 * core + q), core, q, device).start()

            @pl.when(self.at_last)
            def _():
                hop(5, self.piece(3), self.via_2, at(section(y, self.up), l, xq, c), self.base).start()
                for k in (1, 2, 0):
                    device = at(section(self.column(k), 0), l, xq, c)
                    pltpu.make_async_remote_copy(
                        src_ref=self.piece(k), dst_ref=self.via_1,
                        send_sem=hop_send.at[self.base + k], recv_sem=hop_recv.at[self.base + 4],
                        device_id=device, device_id_type=MESH,
                    ).start()

        def along_z(self):
            @pl.when(jnp.logical_not(self.at_last))
            def _():
                self.wait(4, self.via_1)

                @pl.when(self.at_first)
                def _():
                    device = at(section(y, self.up), l, xq, 0)
                    hop_to = self.rows.at[mine, A]
                    pltpu.make_async_remote_copy(
                        src_ref=self.via_1, dst_ref=hop_to, send_sem=hop_send.at[self.base + 5],
                        recv_sem=hop_recv.at[self.base + c],
                        device_id=device, device_id_type=MESH,
                    ).start()

                @pl.when(jnp.logical_not(self.at_first))
                def _():
                    hop(5, self.via_1, self.via_2, at(section(y, self.up), l, xq, c), self.base).start()

        def along_y(self):
            k = self.column(y)
            core = lax.div(k, 2)
            q = lax.rem(k, 2)
            self.wait(5, self.via_2)
            cols = pl.ds(pl.multiple_of(q * QUART, 128), QUART)
            pltpu.make_async_remote_copy(
                src_ref=self.via_2, dst_ref=self.rows.at[mine, cols], send_sem=hop_send.at[self.base + 4],
                recv_sem=hop_recv.at[self.base + 2 * q + lax.rem(c + core, 2)],
                device_id=at(section(self.first, 0), l, xq, core), device_id_type=MESH,
            ).start()

        def wait(self, k, ref):
            hop(k, ref, ref, partner, self.base).wait_recv()

        def arrived(self, q):
            for d in (0, 1):
                hop(2 * q + d, self.rows.at[mine, cols_of(q)], self.rows.at[mine, cols_of(q)], partner, self.base).wait_recv()

        def finish(self):
            for k in (0, 1, 2, 5):
                hop(k, self.via_1, self.via_1, partner, self.base).wait_send()

            @pl.when(jnp.logical_not(self.at_last))
            def _():
                hop(3, self.via_1, self.via_1, partner, self.base).wait_send()

            @pl.when(jnp.logical_not(self.at_first))
            def _():
                hop(4, self.via_2, self.via_2, partner, self.base).wait_send()

    stream_f = Stream(act_ref, hop_f, via_f1, via_f2, 0, 0, 1, lambda v: v)
    stream_b = Stream(cot_ref, hop_b, via_b1, via_b2, 6, 3, -1, lambda v: 3 - v)
    stream_f.start()
    stream_b.start()
    meta_copy = remote(meta_o, meta_p, partner)
    weights_other = []
    for s in (0, 1):
        weights_other.append(
            remote(win_ref.at[0, s, half_of(1 - c)], win.at[:, (2 + s) * HID:(3 + s) * HID], partner)
        )
    weights_other.append(remote(wdn_ref.at[0, :, half_of(1 - c)], wd.at[HID:2 * HID], partner))
    stash_other = remote(stash_ref.at[0], st.at[:, HID:2 * HID], partner)

    stream_f.along_z()
    stream_b.along_z()

    meta_copy.wait_recv()
    meta_c[...] = meta_o[...] + meta_p[...]

    def first_slots(meta, row):
        j = iota((32, 64), 0)
        lane = iota((32, 64), 1)
        core = (j >= CAP).astype(jnp.int32)
        wanted = (j - CAP * core + 1).astype(F32)
        same = (lane >= TOK).astype(jnp.int32) == core
        return [
            jnp.where((meta[row + e:row + e + 1, 0:64] == wanted) & same, 1.0, 0.0).astype(F32)
            for e in range(EXPERTS)
        ]

    def last_slots(meta, row, rows):
        r = iota((rows, 64), 0)
        lane = iota((rows, 64), 1)
        wanted = ((r & 3) + (32 - CAP + 1)).astype(F32)
        return [
            jnp.where((meta[row + e:row + e + 1, 0:64] == wanted) & (lane >= TOK), 1.0, 0.0).astype(F32)
            for e in range(EXPERTS)
        ]

    def selectors(meta, row, weigh):
        a = first_slots(meta, row)
        b = last_slots(meta, row, 16)
        sel_a = jnp.concatenate(a, axis=0)
        sel_b = jnp.concatenate(b, axis=0)
        gate_a = gate_b = None
        if weigh:
            gates = [meta[row + 8 + e:row + 9 + e, 0:64] for e in range(EXPERTS)]
            gate_a = jnp.sum(jnp.concatenate([v * w for v, w in zip(a, gates)], axis=0), axis=1, keepdims=True)
            gate_b = jnp.sum(jnp.concatenate([v * w for v, w in zip(b, gates)], axis=0), axis=1, keepdims=True)
        piece = (iota((64, 64), 0) >> 2) & 3
        parts = [jnp.where(piece == k, sel_b, 0.0).astype(BF16) for k in range(4)]
        return sel_a.astype(BF16), parts, gate_a, gate_b

    def chosen_rows(tables, q, hop, sa, sl):
        sel_a, parts, gate_a, gate_b = tables
        got = jnp.dot(sel_a, hop[:, cols_of(q)], preferred_element_type=F32)
        if gate_a is not None:
            got = got * gate_a
        sa[:, cols_of(q)] = got.astype(BF16)
        for t in range(2):
            total = None
            for k in range(4):
                if t * 128 < piece_width(k):
                    low = q * QUART + k * PIECE + t * 128
                    got = jnp.dot(parts[k], hop[:, low:low + 128], preferred_element_type=F32)
                    total = got if total is None else total + got
            if gate_b is not None:
                total = total * gate_b
            sl[:, q * PIECE + t * 128:q * PIECE + (t + 1) * 128] = total.astype(BF16)

    rows_here = pl.ds(pl.multiple_of(l * 32, 32), 32)
    last_here = pl.ds(pl.multiple_of(l * 16, 16), 16)

    def last_cols(q):
        return slice(q * PIECE, (q + 1) * PIECE)

    def exchange(q, sa, sl, rows, last):
        out = []
        for d in (2, 1, 3):
            e = zdev(d)
            device = at(p, e, xq, c)
            theirs = pl.ds(pl.multiple_of(e * 32, 32), 32)
            last_theirs = pl.ds(pl.multiple_of(e * 16, 16), 16)
            out.append(remote(sa.at[theirs, cols_of(q)], rows.at[rows_here, cols_of(q)], device))
            out.append(remote(sl.at[last_theirs, last_cols(q)], last.at[last_here, last_cols(q)], device))
        own = [
            here(sa.at[rows_here, cols_of(q)], rows.at[rows_here, cols_of(q)]),
            here(sl.at[last_here, last_cols(q)], last.at[last_here, last_cols(q)]),
        ]
        return out, own

    def arrived(copies):
        for copy in copies[0]:
            copy.wait_recv()
        for copy in copies[1]:
            copy.wait()

    def spread_last(q, last, rows):
        m = iota((16, 64), 0)
        n = iota((16, 64), 1)
        for k in range(4):
            width = piece_width(k)
            place = (m >> 2) * 16 + 4 * k + (m & 3)
            pick = jnp.where(n == place, 1.0, 0.0).astype(BF16)
            got = jnp.dot(pick, last[:, q * PIECE:q * PIECE + width], preferred_element_type=F32)
            low = q * QUART + k * PIECE
            rows[128:BLOCK, low:low + width] = got.astype(BF16)

    def block(k):
        return slice(k * BLOCK, (k + 1) * BLOCK)

    def gather_start(q, x):
        to_right = remote(x.at[block(0), cols_of(q)], x.at[block(1), cols_of(q)], right)
        to_left = remote(x.at[block(0), cols_of(q)], x.at[block(2), cols_of(q)], left)
        return [to_right, to_left]

    def gather_forward(q, x, copies):
        copies[q].wait_recv()
        if q == 0:
            return remote(x.at[block(1), A], x.at[block(3), A], right)
        return remote(x.at[block(2), B], x.at[block(3), B], left)

    def permuted(source, target):
        for k, step in enumerate((0, 3, 1, 2)):
            m = iota((BLOCK, SLOTS), 0)
            n = iota((BLOCK, SLOTS), 1)
            at_x = lax.rem(xq + step, 4)
            early = (m >> 5) * BLOCK + (m & 31)
            late = ((m - 128) >> 2) * BLOCK + 32 + (m & 3)
            origin = jnp.where(m < 128, early, late) + at_x * 36
            pick = jnp.where(n == origin, 1.0, 0.0).astype(BF16)
            sp32[block(k)] = jnp.dot(pick, source[...], preferred_element_type=F32)
        target[...] = sp32[...].T.astype(BF16)

    tables = selectors(meta_c, 0, False)
    to_f = []

    @pl.when(stream_f.at_first)
    def _():
        stream_b.along_y()

    for q in (0, 1):
        stream_f.arrived(q)
        chosen_rows(tables, q, hop_f, sa_f, sl_f)
        to_f.append(exchange(q, sa_f, sl_f, x_f, lr_f))

    @pl.when(jnp.logical_not(stream_f.at_first))
    def _():
        stream_f.along_y()

        @pl.when(jnp.logical_not(stream_b.at_first))
        def _():
            stream_b.along_y()

    mirror_meta = remote(meta_c, meta_m, mirror)
    mirror_rows = []
    tables = selectors(meta_c, 16, True)
    for q in (0, 1):
        stream_b.arrived(q)
        mirror_rows.append(remote(hop_b.at[:, cols_of(q)], hop_m.at[:, cols_of(q)], mirror))
        chosen_rows(tables, q, hop_b, sa_b, sl_b)

    ag_f = []
    arrived(to_f[0])
    spread_last(0, lr_f, x_f)
    ag_f.append(gather_start(0, x_f))
    to_b = [exchange(0, sa_b, sl_b, x_b, lr_b)]
    arrived(to_f[1])
    spread_last(1, lr_f, x_f)
    ag_f.append(gather_start(1, x_f))
    to_b.append(exchange(1, sa_b, sl_b, x_b, lr_b))

    for copy in weights:
        copy.wait()
    for copy in weights_other:
        copy.wait_recv()

    def project(k):
        pre[block(k)] = jnp.dot(x_f[block(k)], win[...], preferred_element_type=F32)
        return remote(pre.at[block(k), 2 * HID:4 * HID], pre_r.at[block(k)], partner)

    def activate(k, copy):
        copy.wait_recv()
        gate = pre[block(k), 0:HID] + pre_r[block(k), 0:HID]
        up = pre[block(k), HID:2 * HID] + pre_r[block(k), HID:2 * HID]
        hid[block(k), 0:HID] = (gate / (1.0 + jnp.exp(-gate)) * up).astype(BF16)
        return remote(hid.at[block(k), 0:HID], hid.at[block(k), HID:2 * HID], partner)

    def down(k, copy):
        copy.wait_recv()

        @pl.loop(0, 7)
        def _(t):
            cols = pl.ds(pl.multiple_of(t * 256, 256), 256)
            got = jnp.dot(hid[block(k)], wd[:, cols], preferred_element_type=F32)
            po32[block(k), cols] = got
            po[block(k), cols] = got.astype(BF16)

    pre_0 = project(0)
    ag_f.append(gather_forward(0, x_f, ag_f[0]))
    ag_f.append(gather_forward(1, x_f, ag_f[1]))
    hid_0 = activate(0, pre_0)
    stash_own.wait()
    stash_other.wait_recv()
    permuted(st, spt)

    ag_b = []
    for q in (0, 1):
        arrived(to_b[q])
        spread_last(q, lr_b, x_b)
        ag_b.append(gather_start(q, x_b))
    mirror_stash = remote(stash_ref.at[0], stm.at[:, 0:HID], mirror)

    ag_f[0][1].wait_recv()
    ag_f[1][0].wait_recv()
    pre_1 = project(1)
    pre_2 = project(2)
    hid_1 = activate(1, pre_1)
    hid_2 = activate(2, pre_2)
    down(1, hid_1)
    to_left_a = remote(po.at[block(1), A], r_r.at[:, A], left)
    down(2, hid_2)
    to_right_b = remote(po.at[block(2), B], r_l.at[:, B], right)
    ag_f[2].wait_recv()
    ag_f[3].wait_recv()
    pre_3 = project(3)
    hid_3 = activate(3, pre_3)
    down(3, hid_3)
    opp_a = remote(po.at[block(3), A], r_opp_l, right)
    opp_b = remote(po.at[block(3), B], r_opp_r, left)
    down(0, hid_0)

    mirror_meta.wait_recv()
    tables = selectors(meta_m, 16, True)
    to_m = []
    for q in (0, 1):
        mirror_rows[q].wait_recv()
        chosen_rows(tables, q, hop_m, sa_m, sl_m)
        to_m.append(exchange(q, sa_m, sl_m, x_m, lr_m))

    ag_b.append(gather_forward(0, x_b, ag_b[0]))
    ag_b.append(gather_forward(1, x_b, ag_b[1]))

    opp_a.wait_recv()
    acc_r[...] = (po32[block(2), A] + r_opp_l[...].astype(F32)).astype(BF16)
    to_right_a = remote(acc_r, r_l.at[:, A], right)
    opp_b.wait_recv()
    acc_l[...] = (po32[block(1), B] + r_opp_r[...].astype(F32)).astype(BF16)
    to_left_b = remote(acc_l, r_r.at[:, B], left)


    ag_m = []
    for q in (0, 1):
        arrived(to_m[q])
        spread_last(q, lr_m, x_m)
        ag_m.append(gather_start(q, x_m))

    to_r = []
    m = iota((64, 16), 0)
    n = iota((64, 16), 1)
    place = (m >> 4) * 4 + (m & 3)
    packs = [jnp.where((n == place) & (((m >> 2) & 3) == k), 1.0, 0.0).astype(BF16) for k in range(4)]
    for q, waited in ((0, (to_left_a, to_right_a)), (1, (to_right_b, to_left_b))):
        for copy in waited:
            copy.wait_recv()
        total = po32[block(0), cols_of(q)] + r_l[:, cols_of(q)].astype(F32) + r_r[:, cols_of(q)].astype(F32)
        ret[:, cols_of(q)] = total.astype(BF16)
        for t in range(2):
            total = None
            for k in range(4):
                if t * 128 < piece_width(k):
                    low = q * QUART + k * PIECE + t * 128
                    got = jnp.dot(packs[k], ret[128:BLOCK, low:low + 128], preferred_element_type=F32)
                    total = got if total is None else total + got
            ret_l[:, q * PIECE + t * 128:q * PIECE + (t + 1) * 128] = total.astype(BF16)
        to_r.append(exchange(q, ret, ret_l, rows_r, lr_r))

    mirror_stash.wait_recv()
    stash_pass = remote(stm.at[:, 0:HID], stm.at[:, HID:2 * HID], partner)
    stash_pass.wait_recv()
    permuted(stm, spmt)
    ag_m.append(gather_forward(0, x_m, ag_m[0]))
    ag_m.append(gather_forward(1, x_m, ag_m[1]))

    ag_b[0][1].wait_recv()
    ag_b[1][0].wait_recv()
    ag_b[2].wait_recv()
    ag_b[3].wait_recv()

    @pl.loop(0, 7)
    def _(t):
        cols = pl.ds(pl.multiple_of(t * 256, 256), 256)
        own_g[:, cols] = jnp.dot(spt[...], x_b[:, cols], preferred_element_type=F32).astype(BF16)

    gates = [meta_c[8 + e:9 + e, 0:64] for e in range(EXPERTS)]
    table = [v * w for v, w in zip(first_slots(meta_c, 0), gates)]
    late = last_slots(meta_c, 0, 16)
    row = iota((16, 64), 0) >> 2
    tail = None
    for e in range(EXPERTS):
        part = jnp.where(row == e, late[e] * gates[e], 0.0)
        tail = part if tail is None else tail + part
    table = jnp.concatenate(table + [tail], axis=0).T
    table_hi = table.astype(BF16)
    table_lo = (table - table_hi.astype(F32)).astype(BF16)
    theirs = pl.ds(pl.multiple_of((1 - c) * TOK, TOK), TOK)
    moe_other = []
    moe_own = []
    for q in (0, 1):
        arrived(to_r[q])
        spread_last(q, lr_r, rows_r)
        got = jnp.dot(table_hi, rows_r[:, cols_of(q)], preferred_element_type=F32)
        got += jnp.dot(table_lo, rows_r[:, cols_of(q)], preferred_element_type=F32)
        mo[:, cols_of(q)] = got.astype(BF16)
        moe_other.append(remote(mo.at[theirs, cols_of(q)], moe_ref.at[0, :, quarter_of(c, q)], partner))
        moe_own.append(here(mo.at[mine, cols_of(q)], moe_ref.at[0, :, quarter_of(c, q)]))

    ag_m[0][1].wait_recv()
    ag_m[1][0].wait_recv()
    ag_m[2].wait_recv()
    ag_m[3].wait_recv()

    @pl.loop(0, 7)
    def _(t):
        cols = pl.ds(pl.multiple_of(t * 256, 256), 256)
        other = jnp.dot(spmt[...], x_m[:, cols], preferred_element_type=F32).astype(BF16)
        g[:, cols] = (own_g[:, cols].astype(F32) + other.astype(F32)).astype(BF16)

    grad_other = remote(g.at[HID:2 * HID], grad_ref.at[0, :, half_of(c)], partner)
    grad_own = here(g.at[0:HID], grad_ref.at[0, :, half_of(c)])

    for copy in moe_own + [grad_own]:
        copy.wait()
    for copy in moe_other + [grad_other]:
        copy.wait_recv()
    for copy in sent:
        copy.wait_send()
    stream_f.finish()
    stream_b.finish()


def shards(act_fwd, cot_bwd, routes_fwd, gates_fwd, routes_bwd, gates_bwd, w_in, w_down, stash):
    V = pltpu.VMEM
    scratch = [
        V((32, 128), F32), V((32, 128), F32), V((32, 128), F32), V((32, 128), F32),
        V((64, HALF), BF16), V((64, HALF), BF16), V((64, HALF), BF16),
        V((TOK, QUART), BF16), V((TOK, QUART), BF16), V((TOK, QUART), BF16), V((TOK, QUART), BF16),
        V((128, HALF), BF16), V((128, HALF), BF16), V((128, HALF), BF16),
        V((64, 2 * PIECE), BF16), V((64, 2 * PIECE), BF16), V((64, 2 * PIECE), BF16),
        V((64, 2 * PIECE), BF16), V((64, 2 * PIECE), BF16), V((64, 2 * PIECE), BF16), V((64, 2 * PIECE), BF16),
        V((SLOTS, HALF), BF16), V((SLOTS, HALF), BF16), V((SLOTS, HALF), BF16),
        V((HALF, 4 * HID), BF16), V((2 * HID, HALF), BF16),
        V((SLOTS, 2 * HID), BF16), V((SLOTS, 2 * HID), BF16),
        V((SLOTS, 2 * HID), F32), V((2 * HID, SLOTS), BF16), V((2 * HID, SLOTS), BF16),
        V((SLOTS, 4 * HID), F32), V((SLOTS, 2 * HID), F32), V((SLOTS, 2 * HID), BF16),
        V((SLOTS, HALF), F32), V((SLOTS, HALF), BF16),
        V((BLOCK, QUART), BF16), V((BLOCK, QUART), BF16), V((BLOCK, QUART), BF16), V((BLOCK, QUART), BF16),
        V((BLOCK, HALF), BF16), V((BLOCK, HALF), BF16),
        V((BLOCK, HALF), BF16), V((64, 2 * PIECE), BF16), V((BLOCK, HALF), BF16),
        V((64, HALF), BF16), V((2 * HID, HALF), BF16), V((2 * HID, HALF), BF16),
        pltpu.SemaphoreType.DMA((128,)), pltpu.SemaphoreType.DMA((128,)), pltpu.SemaphoreType.DMA((32,)),
        pltpu.SemaphoreType.DMA((12,)), pltpu.SemaphoreType.DMA((12,)),
    ]
    hbm = pl.BlockSpec(memory_space=pltpu.HBM)
    return pl.pallas_call(
        kernel,
        out_shape=(
            jax.ShapeDtypeStruct((1, TOK, D), BF16),
            jax.ShapeDtypeStruct((1, HID, D), BF16),
        ),
        in_specs=[pl.BlockSpec(memory_space=pltpu.VMEM)] * 4 + [hbm] * 5,
        out_specs=(hbm, hbm),
        scratch_shapes=scratch,
        compiler_params=pltpu.CompilerParams(
            collective_id=0, has_side_effects=True, vmem_limit_bytes=56 * 1024 * 1024
        ),
    )(
        routes_fwd[0].T, gates_fwd[0].T, routes_bwd[0].T, gates_bwd[0].T,
        act_fwd, cot_bwd, w_in, w_down, stash,
    )


def solution(mesh):
    rows = P("pipe", "expert", None)
    in_specs = (rows, rows, rows, rows, rows, rows, P("pipe", None, None, "expert"), rows, rows)
    return jax.shard_map(shards, mesh=mesh, in_specs=in_specs, out_specs=(rows, rows), check_vma=False)
```

time: 154 us -> 129 us (0.84)
  the two profiles are of different devices: /device:TPU:35 before, /device:TPU:1 now
where the time goes in v2:
time: 129 us
  Pallas kernels  125 us (97%)
  local copies, waits for them, and re-layouts  3.8 us (3%)
    pallas_call x1, Pallas kernels, shards(): pl.pallas_call(kernel, out_shape=(jax.ShapeDtypeStruct((1, TOK, D), BF16)...  125 us
    unnamed x2, local copies, waits for them, and re-layouts  3.8 us

profile of v2, /device:TPU:1, one launch (start us, length us, event | category | flops | bytes accessed | tf_op | source)
XLA Modules:
  0.0 129.1 jit_solution(3347414106082350332)
XLA Ops:
  0.6 124.7 %shard_map.104 = (bf16[1,32,3584]{2,1,0:T(8,128)(2,1)}, bf16[1,128,3584]{2,1,0:T(8,128)(2,1)}) custom-call(s32[2,32]{1,0:T(2,128)} %bitcast.12, f32[2,32]{1,0:T(2,128)} %bitcast.13, s32[2,32]{1,0:T(2,128)} %bitcast.14, f32[2,32]{1,0:T(2,128)} %bitcast.15, bf16[1,32,3584]{2,1,0:T(8,128)(2,1)} %act_ref.1, bf16[1,32,3584]{2,1,0:T(8,128)(2,1)} %cot_ref.1, ...), custom_call_target="tpu_custom_call" | custom-call | tf_op jit(solution)/shard_map/pallas_call | solution.py:595
  125.3 1.6 %copy.13 = bf16[1,32,3584]{2,1,0:T(8,128)(2,1)} copy(bf16[1,32,3584]{2,1,0:T(8,128)(2,1)} %get-tuple-element.4) | data formatting | bytes 458752
  127.0 2.2 %copy.14 = bf16[1,128,3584]{2,1,0:T(8,128)(2,1)} copy(bf16[1,128,3584]{2,1,0:T(8,128)(2,1)} %get-tuple-element.5) | data formatting | bytes 1835008

commit v3 on v2

--- a/solution.py
+++ b/solution.py
@@ -36,7 +36,7 @@
     sa_f, sa_b, sa_m, sl_f, sl_b, sl_m,
     lr_f, lr_b, lr_m, lr_r,
     x_f, x_b, x_m,
-    win, wd, st, stm, sp32, spt, spmt,
+    win, wd, st, stm, sp32, spt, spmt, spm_last,
     pre, pre_r, hid,
     po32, po, r_opp_l, r_opp_r, acc_r, acc_l, r_l, r_r,
     ret, ret_l, rows_r, mo, own_g, g,
@@ -126,14 +126,6 @@
             weight, place, precision=lax.Precision.HIGHEST, preferred_element_type=F32
         )
 
-    table_rows(route_f_ref, gate_f_ref, 0)
-    table_rows(route_b_ref, gate_b_ref, 16)
-    weights = []
-    for s in (0, 1):
-        weights.append(here(win_ref.at[0, s, half_of(c)], win.at[:, s * HID:(s + 1) * HID]))
-    weights.append(here(wdn_ref.at[0, :, half_of(c)], wd.at[0:HID]))
-    stash_own = here(stash_ref.at[0], st.at[:, 0:HID])
-
     pl.semaphore_wait(barrier, len(greeted))
 
     def hop(k, src, dst, device, base):
@@ -232,6 +224,13 @@
     stream_b = Stream(cot_ref, hop_b, via_b1, via_b2, 6, 3, -1, lambda v: 3 - v)
     stream_f.start()
     stream_b.start()
+    table_rows(route_f_ref, gate_f_ref, 0)
+    table_rows(route_b_ref, gate_b_ref, 16)
+    weights = []
+    for s in (0, 1):
+        weights.append(here(win_ref.at[0, s, half_of(c)], win.at[:, s * HID:(s + 1) * HID]))
+    weights.append(here(wdn_ref.at[0, :, half_of(c)], wd.at[0:HID]))
+    stash_own = here(stash_ref.at[0], st.at[:, 0:HID])
     meta_copy = remote(meta_o, meta_p, partner)
     weights_other = []
     for s in (0, 1):
@@ -309,13 +308,26 @@
         for d in (2, 1, 3):
             e = zdev(d)
             device = at(p, e, xq, c)
+            k = 4 - d
             theirs = pl.ds(pl.multiple_of(e * 32, 32), 32)
             last_theirs = pl.ds(pl.multiple_of(e * 16, 16), 16)
-            out.append(remote(sa.at[theirs, cols_of(q)], rows.at[rows_here, cols_of(q)], device))
-            out.append(remote(sl.at[last_theirs, last_cols(q)], last.at[last_here, last_cols(q)], device))
+            out.append(remote(sa.at[theirs, cols_of(q)], rows.at[k * 32:(k + 1) * 32, cols_of(q)], device))
+            out.append(remote(sl.at[last_theirs, last_cols(q)], last.at[k * 16:(k + 1) * 16, last_cols(q)], device))
         own = [
-            here(sa.at[rows_here, cols_of(q)], rows.at[rows_here, cols_of(q)]),
-            here(sl.at[last_here, last_cols(q)], last.at[last_here, last_cols(q)]),
+            here(sa.at[rows_here, cols_of(q)], rows.at[0:32, cols_of(q)]),
+            here(sl.at[last_here, last_cols(q)], last.at[0:16, last_cols(q)]),
+        ]
+        return out, own
+
+    def exchange_back(q, rows, last, back, back_last):
+        out = []
+        for d in (2, 1, 3):
+            device = at(p, zdev(d), xq, c)
+            out.append(remote(rows.at[d * 32:(d + 1) * 32, cols_of(q)], back.at[rows_here, cols_of(q)], device))
+            out.append(remote(last.at[d * 16:(d + 1) * 16, last_cols(q)], back_last.at[last_here, last_cols(q)], device))
+        own = [
+            here(rows.at[0:32, cols_of(q)], back.at[rows_here, cols_of(q)]),
+            here(last.at[0:16, last_cols(q)], back_last.at[last_here, last_cols(q)]),
         ]
         return out, own
 
@@ -339,31 +351,56 @@
     def block(k):
         return slice(k * BLOCK, (k + 1) * BLOCK)
 
-    def gather_start(q, x):
-        to_right = remote(x.at[block(0), cols_of(q)], x.at[block(1), cols_of(q)], right)
-        to_left = remote(x.at[block(0), cols_of(q)], x.at[block(2), cols_of(q)], left)
-        return [to_right, to_left]
-
-    def gather_forward(q, x, copies):
-        copies[q].wait_recv()
-        if q == 0:
-            return remote(x.at[block(1), A], x.at[block(3), A], right)
-        return remote(x.at[block(2), B], x.at[block(3), B], left)
-
-    def permuted(source, target):
+    def part(k, n):
+        return slice(k * BLOCK, k * BLOCK + 32) if n == 0 else slice(k * BLOCK + 32, (k + 1) * BLOCK)
+
+    class Gather:
+        def __init__(self, x, sa):
+            self.x, self.sa = x, sa
+            self.copies = {}
+
+        def start(self, n, q):
+            x = self.x
+            src = self.sa.at[rows_here, cols_of(q)] if n == 0 else x.at[part(0, 1), cols_of(q)]
+            sides = [(1, right), (2, left)]
+            for k, device in sides if q == 0 else sides[::-1]:
+                self.copies[n, q, k] = remote(src, x.at[part(k, n), cols_of(q)], device)
+
+        def forward(self, n):
+            x = self.x
+            for q, k, device in ((0, 1, right), (1, 2, left)):
+                self.copies[n, q, k].wait_recv()
+                self.copies[n, q, 3] = remote(x.at[part(k, n), cols_of(q)], x.at[part(3, n), cols_of(q)], device)
+
+        def near(self):
+            for n in (0, 1):
+                self.copies[n, 0, 2].wait_recv()
+                self.copies[n, 1, 1].wait_recv()
+
+        def far(self, *halves):
+            for q in halves or (0, 1):
+                self.copies[0, q, 3].wait_recv()
+                self.copies[1, q, 3].wait_recv()
+
+    def permuted(source, target, last=None):
         for k, step in enumerate((0, 3, 1, 2)):
             m = iota((BLOCK, SLOTS), 0)
             n = iota((BLOCK, SLOTS), 1)
             at_x = lax.rem(xq + step, 4)
-            early = (m >> 5) * BLOCK + (m & 31)
-            late = ((m - 128) >> 2) * BLOCK + 32 + (m & 3)
+            early = ((l + (m >> 5)) & 3) * BLOCK + (m & 31)
+            late = ((l + ((m - 128) >> 2)) & 3) * BLOCK + 32 + (m & 3)
             origin = jnp.where(m < 128, early, late) + at_x * 36
             pick = jnp.where(n == origin, 1.0, 0.0).astype(BF16)
             sp32[block(k)] = jnp.dot(pick, source[...], preferred_element_type=F32)
         target[...] = sp32[...].T.astype(BF16)
+        if last is not None:
+            last[...] = sp32[block(3)].T.astype(BF16)
 
     tables = selectors(meta_c, 0, False)
     to_f = []
+    ag_f = Gather(x_f, sa_f)
+    ag_b = Gather(x_b, sa_b)
+    ag_m = Gather(x_m, sa_m)
 
     @pl.when(stream_f.at_first)
     def _():
@@ -373,6 +410,7 @@
         stream_f.arrived(q)
         chosen_rows(tables, q, hop_f, sa_f, sl_f)
         to_f.append(exchange(q, sa_f, sl_f, x_f, lr_f))
+        ag_f.start(0, q)
 
     @pl.when(jnp.logical_not(stream_f.at_first))
     def _():
@@ -382,83 +420,82 @@
         def _():
             stream_b.along_y()
 
-    mirror_meta = remote(meta_c, meta_m, mirror)
-    mirror_rows = []
     tables = selectors(meta_c, 16, True)
     for q in (0, 1):
         stream_b.arrived(q)
-        mirror_rows.append(remote(hop_b.at[:, cols_of(q)], hop_m.at[:, cols_of(q)], mirror))
         chosen_rows(tables, q, hop_b, sa_b, sl_b)
-
-    ag_f = []
-    arrived(to_f[0])
-    spread_last(0, lr_f, x_f)
-    ag_f.append(gather_start(0, x_f))
-    to_b = [exchange(0, sa_b, sl_b, x_b, lr_b)]
-    arrived(to_f[1])
-    spread_last(1, lr_f, x_f)
-    ag_f.append(gather_start(1, x_f))
-    to_b.append(exchange(1, sa_b, sl_b, x_b, lr_b))
+        ag_b.start(0, q)
+
+    ag_f.forward(0)
+    to_b = []
+    for q in (0, 1):
+        arrived(to_f[q])
+        spread_last(q, lr_f, x_f)
+        ag_f.start(1, q)
+        to_b.append(exchange(q, sa_b, sl_b, x_b, lr_b))
+    ag_b.forward(0)
 
     for copy in weights:
         copy.wait()
     for copy in weights_other:
         copy.wait_recv()
 
-    def project(k):
-        pre[block(k)] = jnp.dot(x_f[block(k)], win[...], preferred_element_type=F32)
-        return remote(pre.at[block(k), 2 * HID:4 * HID], pre_r.at[block(k)], partner)
-
-    def activate(k, copy):
+    def blocks(k, n):
+        return slice(k * BLOCK, (k + n) * BLOCK)
+
+    def project(k, n):
+        rows = blocks(k, n)
+        pre[rows] = jnp.dot(x_f[rows], win[...], preferred_element_type=F32)
+        return remote(pre.at[rows, 2 * HID:4 * HID], pre_r.at[rows], partner)
+
+    def activate(k, n, copy):
+        rows = blocks(k, n)
         copy.wait_recv()
-        gate = pre[block(k), 0:HID] + pre_r[block(k), 0:HID]
-        up = pre[block(k), HID:2 * HID] + pre_r[block(k), HID:2 * HID]
-        hid[block(k), 0:HID] = (gate / (1.0 + jnp.exp(-gate)) * up).astype(BF16)
-        return remote(hid.at[block(k), 0:HID], hid.at[block(k), HID:2 * HID], partner)
-
-    def down(k, copy):
-        copy.wait_recv()
+        gate = pre[rows, 0:HID] + pre_r[rows, 0:HID]
+        up = pre[rows, HID:2 * HID] + pre_r[rows, HID:2 * HID]
+        hid[rows, 0:HID] = (gate / (1.0 + jnp.exp(-gate)) * up).astype(BF16)
+        return remote(hid.at[rows, 0:HID], hid.at[rows, HID:2 * HID], partner)
+
+    def down(k, n):
+        rows = blocks(k, n)
 
         @pl.loop(0, 7)
         def _(t):
             cols = pl.ds(pl.multiple_of(t * 256, 256), 256)
-            got = jnp.dot(hid[block(k)], wd[:, cols], preferred_element_type=F32)
-            po32[block(k), cols] = got
-            po[block(k), cols] = got.astype(BF16)
-
-    pre_0 = project(0)
-    ag_f.append(gather_forward(0, x_f, ag_f[0]))
-    ag_f.append(gather_forward(1, x_f, ag_f[1]))
-    hid_0 = activate(0, pre_0)
+            got = jnp.dot(hid[rows], wd[:, cols], preferred_element_type=F32)
+            po32[rows, cols] = got
+            po[rows, cols] = got.astype(BF16)
+
+    mirror_meta = remote(meta_c, meta_m, mirror)
+    mirror_rows = [remote(hop_b.at[:, cols_of(q)], hop_m.at[:, cols_of(q)], mirror) for q in (0, 1)]
+    pre_0 = project(0, 1)
+    ag_f.forward(1)
+    hid_0 = activate(0, 1, pre_0)
     stash_own.wait()
     stash_other.wait_recv()
     permuted(st, spt)
 
-    ag_b = []
     for q in (0, 1):
         arrived(to_b[q])
         spread_last(q, lr_b, x_b)
-        ag_b.append(gather_start(q, x_b))
-    mirror_stash = remote(stash_ref.at[0], stm.at[:, 0:HID], mirror)
-
-    ag_f[0][1].wait_recv()
-    ag_f[1][0].wait_recv()
-    pre_1 = project(1)
-    pre_2 = project(2)
-    hid_1 = activate(1, pre_1)
-    hid_2 = activate(2, pre_2)
-    down(1, hid_1)
+        ag_b.start(1, q)
+
+    ag_f.near()
+    pre_1 = project(1, 2)
+    hid_1 = activate(1, 2, pre_1)
+    hid_1.wait_recv()
+    down(1, 2)
     to_left_a = remote(po.at[block(1), A], r_r.at[:, A], left)
-    down(2, hid_2)
     to_right_b = remote(po.at[block(2), B], r_l.at[:, B], right)
-    ag_f[2].wait_recv()
-    ag_f[3].wait_recv()
-    pre_3 = project(3)
-    hid_3 = activate(3, pre_3)
-    down(3, hid_3)
+    ag_f.far()
+    pre_3 = project(3, 1)
+    hid_3 = activate(3, 1, pre_3)
+    hid_3.wait_recv()
+    down(3, 1)
     opp_a = remote(po.at[block(3), A], r_opp_l, right)
     opp_b = remote(po.at[block(3), B], r_opp_r, left)
-    down(0, hid_0)
+    hid_0.wait_recv()
+    down(0, 1)
 
     mirror_meta.wait_recv()
     tables = selectors(meta_m, 16, True)
@@ -467,23 +504,17 @@
         mirror_rows[q].wait_recv()
         chosen_rows(tables, q, hop_m, sa_m, sl_m)
         to_m.append(exchange(q, sa_m, sl_m, x_m, lr_m))
-
-    ag_b.append(gather_forward(0, x_b, ag_b[0]))
-    ag_b.append(gather_forward(1, x_b, ag_b[1]))
-
+        ag_m.start(0, q)
+
+    mirror_stash = remote(stash_ref.at[0], stm.at[:, 0:HID], mirror)
     opp_a.wait_recv()
     acc_r[...] = (po32[block(2), A] + r_opp_l[...].astype(F32)).astype(BF16)
     to_right_a = remote(acc_r, r_l.at[:, A], right)
     opp_b.wait_recv()
     acc_l[...] = (po32[block(1), B] + r_opp_r[...].astype(F32)).astype(BF16)
     to_left_b = remote(acc_l, r_r.at[:, B], left)
-
-
-    ag_m = []
-    for q in (0, 1):
-        arrived(to_m[q])
-        spread_last(q, lr_m, x_m)
-        ag_m.append(gather_start(q, x_m))
+    ag_b.forward(1)
+
 
     to_r = []
     m = iota((64, 16), 0)
@@ -503,25 +534,27 @@
                     got = jnp.dot(packs[k], ret[128:BLOCK, low:low + 128], preferred_element_type=F32)
                     total = got if total is None else total + got
             ret_l[:, q * PIECE + t * 128:q * PIECE + (t + 1) * 128] = total.astype(BF16)
-        to_r.append(exchange(q, ret, ret_l, rows_r, lr_r))
-
+        to_r.append(exchange_back(q, ret, ret_l, rows_r, lr_r))
+
+    ag_m.forward(0)
+    for q in (0, 1):
+        arrived(to_m[q])
+        spread_last(q, lr_m, x_m)
+        ag_m.start(1, q)
+    ag_m.forward(1)
     mirror_stash.wait_recv()
     stash_pass = remote(stm.at[:, 0:HID], stm.at[:, HID:2 * HID], partner)
-    stash_pass.wait_recv()
-    permuted(stm, spmt)
-    ag_m.append(gather_forward(0, x_m, ag_m[0]))
-    ag_m.append(gather_forward(1, x_m, ag_m[1]))
-
-    ag_b[0][1].wait_recv()
-    ag_b[1][0].wait_recv()
-    ag_b[2].wait_recv()
-    ag_b[3].wait_recv()
+
+    ag_b.near()
+    ag_b.far()
 
     @pl.loop(0, 7)
     def _(t):
         cols = pl.ds(pl.multiple_of(t * 256, 256), 256)
         own_g[:, cols] = jnp.dot(spt[...], x_b[:, cols], preferred_element_type=F32).astype(BF16)
 
+    stash_pass.wait_recv()
+    permuted(stm, spmt, spm_last)
     gates = [meta_c[8 + e:9 + e, 0:64] for e in range(EXPERTS)]
     table = [v * w for v, w in zip(first_slots(meta_c, 0), gates)]
     late = last_slots(meta_c, 0, 16)
@@ -545,24 +578,36 @@
         moe_other.append(remote(mo.at[theirs, cols_of(q)], moe_ref.at[0, :, quarter_of(c, q)], partner))
         moe_own.append(here(mo.at[mine, cols_of(q)], moe_ref.at[0, :, quarter_of(c, q)]))
 
-    ag_m[0][1].wait_recv()
-    ag_m[1][0].wait_recv()
-    ag_m[2].wait_recv()
-    ag_m[3].wait_recv()
+    ag_m.near()
 
     @pl.loop(0, 7)
     def _(t):
         cols = pl.ds(pl.multiple_of(t * 256, 256), 256)
-        other = jnp.dot(spmt[...], x_m[:, cols], preferred_element_type=F32).astype(BF16)
-        g[:, cols] = (own_g[:, cols].astype(F32) + other.astype(F32)).astype(BF16)
-
-    grad_other = remote(g.at[HID:2 * HID], grad_ref.at[0, :, half_of(c)], partner)
-    grad_own = here(g.at[0:HID], grad_ref.at[0, :, half_of(c)])
-
-    for copy in moe_own + [grad_own]:
+        po32[0:256, cols] = jnp.dot(
+            spmt[:, 0:3 * BLOCK], x_m[0:3 * BLOCK, cols], preferred_element_type=F32
+        )
+
+    grads = []
+    for q in (0, 1):
+        ag_m.far(q)
+
+        @pl.loop(0, 7)
+        def _(t):
+            cols = pl.ds(pl.multiple_of(q * QUART + t * 128, 128), 128)
+            other = jnp.dot(spm_last[...], x_m[block(3), cols], preferred_element_type=F32)
+            other = (po32[0:256, cols] + other).astype(BF16)
+            g[:, cols] = (own_g[:, cols].astype(F32) + other.astype(F32)).astype(BF16)
+
+        there = grad_ref.at[0, :, quarter_of(c, q)]
+        grads.append((remote(g.at[HID:2 * HID, cols_of(q)], there, partner), here(g.at[0:HID, cols_of(q)], there)))
+
+    for copy in moe_own:
         copy.wait()
-    for copy in moe_other + [grad_other]:
+    for copy in moe_other:
         copy.wait_recv()
+    for other, own in grads:
+        own.wait()
+        other.wait_recv()
     for copy in sent:
         copy.wait_send()
     stream_f.finish()
@@ -581,7 +626,7 @@
         V((SLOTS, HALF), BF16), V((SLOTS, HALF), BF16), V((SLOTS, HALF), BF16),
         V((HALF, 4 * HID), BF16), V((2 * HID, HALF), BF16),
         V((SLOTS, 2 * HID), BF16), V((SLOTS, 2 * HID), BF16),
-        V((SLOTS, 2 * HID), F32), V((2 * HID, SLOTS), BF16), V((2 * HID, SLOTS), BF16),
+        V((SLOTS, 2 * HID), F32), V((2 * HID, SLOTS), BF16), V((2 * HID, SLOTS), BF16), V((2 * HID, BLOCK), BF16),
         V((SLOTS, 4 * HID), F32), V((SLOTS, 2 * HID), F32), V((SLOTS, 2 * HID), BF16),
         V((SLOTS, HALF), F32), V((SLOTS, HALF), BF16),
         V((BLOCK, QUART), BF16), V((BLOCK, QUART), BF16), V((BLOCK, QUART), BF16), V((BLOCK, QUART), BF16),

time: 129 us -> 119 us (0.922)
  the two profiles are of different devices: /device:TPU:1 before, /device:TPU:45 now
where the time goes in v3:
time: 119 us
  Pallas kernels  114 us (96%)
  local copies, waits for them, and re-layouts  3.8 us (3%)
    pallas_call x1, Pallas kernels, shards(): pl.pallas_call(kernel, out_shape=(jax.ShapeDtypeStruct((1, TOK, D), BF16)...  114 us
    unnamed x2, local copies, waits for them, and re-layouts  3.8 us

profile of v3, /device:TPU:45, one launch (start us, length us, event | category | flops | bytes accessed | tf_op | source)
XLA Modules:
  0.0 118.9 jit_solution(8505552461483157327)
XLA Ops:
  0.6 114.4 %shard_map.104 = (bf16[1,32,3584]{2,1,0:T(8,128)(2,1)}, bf16[1,128,3584]{2,1,0:T(8,128)(2,1)}) custom-call(s32[2,32]{1,0:T(2,128)} %bitcast.12, f32[2,32]{1,0:T(2,128)} %bitcast.13, s32[2,32]{1,0:T(2,128)} %bitcast.14, f32[2,32]{1,0:T(2,128)} %bitcast.15, bf16[1,32,3584]{2,1,0:T(8,128)(2,1)} %act_ref.1, bf16[1,32,3584]{2,1,0:T(8,128)(2,1)} %cot_ref.1, ...), custom_call_target="tpu_custom_call" | custom-call | tf_op jit(solution)/shard_map/pallas_call | solution.py:640
  115.1 1.6 %copy.13 = bf16[1,32,3584]{2,1,0:T(8,128)(2,1)} copy(bf16[1,32,3584]{2,1,0:T(8,128)(2,1)} %get-tuple-element.4) | data formatting | bytes 458752
  116.7 2.2 %copy.14 = bf16[1,128,3584]{2,1,0:T(8,128)(2,1)} copy(bf16[1,128,3584]{2,1,0:T(8,128)(2,1)} %get-tuple-element.5) | data formatting | bytes 1835008

commit v4 on v3

--- a/solution.py
+++ b/solution.py
@@ -31,7 +31,7 @@
 def kernel(
     route_f_ref, gate_f_ref, route_b_ref, gate_b_ref, act_ref, cot_ref, win_ref, wdn_ref, stash_ref,
     moe_ref, grad_ref,
-    meta_o, meta_p, meta_c, meta_m,
+    route_f, gate_f, route_b, gate_b, meta_o, meta_p, meta_c, meta_m,
     hop_f, hop_b, hop_m, via_f1, via_f2, via_b1, via_b2,
     sa_f, sa_b, sa_m, sl_f, sl_b, sl_m,
     lr_f, lr_b, lr_m, lr_r,
@@ -40,7 +40,7 @@
     pre, pre_r, hid,
     po32, po, r_opp_l, r_opp_r, acc_r, acc_l, r_l, r_r,
     ret, ret_l, rows_r, mo, own_g, g,
-    send_sem, recv_sem, local_sem, hop_send, hop_recv,
+    send_sem, recv_sem, local_sem, hop_send, hop_recv, small_sem,
 ):
     p = lax.axis_index("pipe")
     i = lax.axis_index("expert")
@@ -67,6 +67,10 @@
     def zdev(d):
         return lax.rem(l + d, 4)
 
+    small = [(route_f_ref, route_f), (gate_f_ref, gate_f), (route_b_ref, route_b), (gate_b_ref, gate_b)]
+    small = [pltpu.make_async_copy(src, dst, small_sem.at[k]) for k, (src, dst) in enumerate(small)]
+    for copy in small:
+        copy.start()
     barrier = pltpu.get_barrier_semaphore()
     greeted = [at(section(lax.rem(y + d, 4), 0), l, xq, cc) for d in (1, 2, 3) for cc in (c, 1 - c)]
     greeted += [at(section(y, up), l, xq, cc) for up in (1, -1) for cc in (c, 1 - c)]
@@ -224,8 +228,10 @@
     stream_b = Stream(cot_ref, hop_b, via_b1, via_b2, 6, 3, -1, lambda v: 3 - v)
     stream_f.start()
     stream_b.start()
-    table_rows(route_f_ref, gate_f_ref, 0)
-    table_rows(route_b_ref, gate_b_ref, 16)
+    for copy in small:
+        copy.wait()
+    table_rows(route_f, gate_f, 0)
+    table_rows(route_b, gate_b, 16)
     weights = []
     for s in (0, 1):
         weights.append(here(win_ref.at[0, s, half_of(c)], win.at[:, s * HID:(s + 1) * HID]))
@@ -433,6 +439,8 @@
         spread_last(q, lr_f, x_f)
         ag_f.start(1, q)
         to_b.append(exchange(q, sa_b, sl_b, x_b, lr_b))
+    mirror_meta = remote(meta_c, meta_m, mirror)
+    mirror_rows = [remote(hop_b.at[:, cols_of(q)], hop_m.at[:, cols_of(q)], mirror) for q in (0, 1)]
     ag_b.forward(0)
 
     for copy in weights:
@@ -466,8 +474,6 @@
             po32[rows, cols] = got
             po[rows, cols] = got.astype(BF16)
 
-    mirror_meta = remote(meta_c, meta_m, mirror)
-    mirror_rows = [remote(hop_b.at[:, cols_of(q)], hop_m.at[:, cols_of(q)], mirror) for q in (0, 1)]
     pre_0 = project(0, 1)
     ag_f.forward(1)
     hid_0 = activate(0, 1, pre_0)
@@ -482,20 +488,18 @@
 
     ag_f.near()
     pre_1 = project(1, 2)
-    hid_1 = activate(1, 2, pre_1)
-    hid_1.wait_recv()
-    down(1, 2)
-    to_left_a = remote(po.at[block(1), A], r_r.at[:, A], left)
-    to_right_b = remote(po.at[block(2), B], r_l.at[:, B], right)
     ag_f.far()
     pre_3 = project(3, 1)
+    hid_1 = activate(1, 2, pre_1)
     hid_3 = activate(3, 1, pre_3)
     hid_3.wait_recv()
     down(3, 1)
     opp_a = remote(po.at[block(3), A], r_opp_l, right)
     opp_b = remote(po.at[block(3), B], r_opp_r, left)
-    hid_0.wait_recv()
-    down(0, 1)
+    hid_1.wait_recv()
+    down(1, 2)
+    to_left_a = remote(po.at[block(1), A], r_r.at[:, A], left)
+    to_right_b = remote(po.at[block(2), B], r_l.at[:, B], right)
 
     mirror_meta.wait_recv()
     tables = selectors(meta_m, 16, True)
@@ -515,6 +519,9 @@
     to_left_b = remote(acc_l, r_r.at[:, B], left)
     ag_b.forward(1)
 
+
+    hid_0.wait_recv()
+    down(0, 1)
 
     to_r = []
     m = iota((64, 16), 0)
@@ -614,9 +621,26 @@
     stream_b.finish()
 
 
+def write(moe_ref, grad_ref, moe_out, grad_out, moe, grad, sems):
+    pieces = [(moe_ref, moe, moe_out)]
+    for k in range(4):
+        rows = slice(k * 32, (k + 1) * 32)
+        pieces.append((grad_ref.at[:, rows], grad.at[:, rows], grad_out.at[:, rows]))
+    loads = [pltpu.make_async_copy(src, held, sems.at[k]) for k, (src, held, _) in enumerate(pieces)]
+    for copy in loads:
+        copy.start()
+    stores = [pltpu.make_async_copy(held, dst, sems.at[k]) for k, (_, held, dst) in enumerate(pieces)]
+    for load, store in zip(loads, stores):
+        load.wait()
+        store.start()
+    for store in stores:
+        store.wait()
+
+
 def shards(act_fwd, cot_bwd, routes_fwd, gates_fwd, routes_bwd, gates_bwd, w_in, w_down, stash):
     V = pltpu.VMEM
     scratch = [
+        V((2, TOK), jnp.int32), V((2, TOK), F32), V((2, TOK), jnp.int32), V((2, TOK), F32),
         V((32, 128), F32), V((32, 128), F32), V((32, 128), F32), V((32, 128), F32),
         V((64, HALF), BF16), V((64, HALF), BF16), V((64, HALF), BF16),
         V((TOK, QUART), BF16), V((TOK, QUART), BF16), V((TOK, QUART), BF16), V((TOK, QUART), BF16),
@@ -635,15 +659,16 @@
         V((64, HALF), BF16), V((2 * HID, HALF), BF16), V((2 * HID, HALF), BF16),
         pltpu.SemaphoreType.DMA((128,)), pltpu.SemaphoreType.DMA((128,)), pltpu.SemaphoreType.DMA((32,)),
         pltpu.SemaphoreType.DMA((12,)), pltpu.SemaphoreType.DMA((12,)),
+        pltpu.SemaphoreType.DMA((4,)),
     ]
     hbm = pl.BlockSpec(memory_space=pltpu.HBM)
-    return pl.pallas_call(
+    results = pl.pallas_call(
         kernel,
         out_shape=(
             jax.ShapeDtypeStruct((1, TOK, D), BF16),
             jax.ShapeDtypeStruct((1, HID, D), BF16),
         ),
-        in_specs=[pl.BlockSpec(memory_space=pltpu.VMEM)] * 4 + [hbm] * 5,
+        in_specs=[hbm] * 9,
         out_specs=(hbm, hbm),
         scratch_shapes=scratch,
         compiler_params=pltpu.CompilerParams(
@@ -653,6 +678,15 @@
         routes_fwd[0].T, gates_fwd[0].T, routes_bwd[0].T, gates_bwd[0].T,
         act_fwd, cot_bwd, w_in, w_down, stash,
     )
+    return pl.pallas_call(
+        write,
+        out_shape=tuple(jax.ShapeDtypeStruct(r.shape, r.dtype) for r in results),
+        in_specs=[hbm, hbm],
+        out_specs=(hbm, hbm),
+        scratch_shapes=[
+            pltpu.VMEM((1, TOK, D), BF16), pltpu.VMEM((1, HID, D), BF16), pltpu.SemaphoreType.DMA((6,)),
+        ],
+    )(*results)
 
 
 def solution(mesh):

time: 119 us -> 116 us (0.975)
  the two profiles are of different devices: /device:TPU:45 before, /device:TPU:1 now
where the time goes in v4:
time: 116 us; the launch traced here: 114 us
  Pallas kernels  113 us (97%)
    pallas_call x1, Pallas kernels, shards(): pl.pallas_call(kernel, out_shape=(jax.ShapeDtypeStruct((1, TOK, D), BF16)...  111 us

profile of v4, /device:TPU:1, one launch (start us, length us, event | category | flops | bytes accessed | tf_op | source)
XLA Modules:
  0.0 114.0 jit_solution(9842774648830498883)
XLA Ops:
  0.6 111.3 %shard_map.104 = (bf16[1,32,3584]{2,1,0:T(8,128)(2,1)}, bf16[1,128,3584]{2,1,0:T(8,128)(2,1)}) custom-call(s32[2,32]{1,0:T(2,128)} %bitcast.12, f32[2,32]{1,0:T(2,128)} %bitcast.13, s32[2,32]{1,0:T(2,128)} %bitcast.14, f32[2,32]{1,0:T(2,128)} %bitcast.15, bf16[1,32,3584]{2,1,0:T(8,128)(2,1)} %act_ref.1, bf16[1,32,3584]{2,1,0:T(8,128)(2,1)} %cot_ref.1, ...), custom_call_target="tpu_custom_call" | custom-call | tf_op jit(solution)/shard_map/pallas_call | solution.py:665
  111.9 2.1 %shard_map.105 = (bf16[1,32,3584]{2,1,0:T(8,128)(2,1)}, bf16[1,128,3584]{2,1,0:T(8,128)(2,1)}) custom-call(bf16[1,32,3584]{2,1,0:T(8,128)(2,1)} %get-tuple-element.4.moe_ref, bf16[1,128,3584]{2,1,0:T(8,128)(2,1)} %get-tuple-element.5.grad_ref), custom_call_target="tpu_custom_call" | custom-call | tf_op jit(solution)/shard_map/pallas_call | solution.py:681

commit v5 on v4

--- a/solution.py
+++ b/solution.py
@@ -510,13 +510,13 @@
         to_m.append(exchange(q, sa_m, sl_m, x_m, lr_m))
         ag_m.start(0, q)
 
-    mirror_stash = remote(stash_ref.at[0], stm.at[:, 0:HID], mirror)
     opp_a.wait_recv()
     acc_r[...] = (po32[block(2), A] + r_opp_l[...].astype(F32)).astype(BF16)
     to_right_a = remote(acc_r, r_l.at[:, A], right)
     opp_b.wait_recv()
     acc_l[...] = (po32[block(1), B] + r_opp_r[...].astype(F32)).astype(BF16)
     to_left_b = remote(acc_l, r_r.at[:, B], left)
+    mirror_stash = remote(stash_ref.at[0], stm.at[:, 0:HID], mirror)
     ag_b.forward(1)
 
 
@@ -548,7 +548,6 @@
         arrived(to_m[q])
         spread_last(q, lr_m, x_m)
         ag_m.start(1, q)
-    ag_m.forward(1)
     mirror_stash.wait_recv()
     stash_pass = remote(stm.at[:, 0:HID], stm.at[:, HID:2 * HID], partner)
 
@@ -568,11 +567,12 @@
     row = iota((16, 64), 0) >> 2
     tail = None
     for e in range(EXPERTS):
-        part = jnp.where(row == e, late[e] * gates[e], 0.0)
-        tail = part if tail is None else tail + part
+        own_part = jnp.where(row == e, late[e] * gates[e], 0.0)
+        tail = own_part if tail is None else tail + own_part
     table = jnp.concatenate(table + [tail], axis=0).T
     table_hi = table.astype(BF16)
     table_lo = (table - table_hi.astype(F32)).astype(BF16)
+    ag_m.forward(1)
     theirs = pl.ds(pl.multiple_of((1 - c) * TOK, TOK), TOK)
     moe_other = []
     moe_own = []

time: 116 us -> 116 us (level)
  no operation moved by 1% of the time
where the time goes in v5:
time: 116 us; the launch traced here: 114 us
  Pallas kernels  113 us (97%)
    pallas_call x1, Pallas kernels, shards(): pl.pallas_call(kernel, out_shape=(jax.ShapeDtypeStruct((1, TOK, D), BF16)...  111 us

profile of v5, /device:TPU:1, one launch (start us, length us, event | category | flops | bytes accessed | tf_op | source)
XLA Modules:
  0.0 114.0 jit_solution(154291768042338938)
XLA Ops:
  0.6 111.3 %shard_map.104 = (bf16[1,32,3584]{2,1,0:T(8,128)(2,1)}, bf16[1,128,3584]{2,1,0:T(8,128)(2,1)}) custom-call(s32[2,32]{1,0:T(2,128)} %bitcast.12, f32[2,32]{1,0:T(2,128)} %bitcast.13, s32[2,32]{1,0:T(2,128)} %bitcast.14, f32[2,32]{1,0:T(2,128)} %bitcast.15, bf16[1,32,3584]{2,1,0:T(8,128)(2,1)} %act_ref.1, bf16[1,32,3584]{2,1,0:T(8,128)(2,1)} %cot_ref.1, ...), custom_call_target="tpu_custom_call" | custom-call | tf_op jit(solution)/shard_map/pallas_call | solution.py:665
  111.9 2.1 %shard_map.105 = (bf16[1,32,3584]{2,1,0:T(8,128)(2,1)}, bf16[1,128,3584]{2,1,0:T(8,128)(2,1)}) custom-call(bf16[1,32,3584]{2,1,0:T(8,128)(2,1)} %get-tuple-element.4.moe_ref, bf16[1,128,3584]{2,1,0:T(8,128)(2,1)} %get-tuple-element.5.grad_ref), custom_call_target="tpu_custom_call" | custom-call | tf_op jit(solution)/shard_map/pallas_call | solution.py:681
